TPU v7x, 256 devices: a whole 4x4x8 slice. The times are simulated.
256 devices in a mesh: hid: 4 (over y), blk: 64 (over x, z, core).
Axes of the slice: x: 4, y: 4, z: 8, core: 2. Of those that a mesh axis runs over, the one named last changes fastest.
Arguments:
- features: bfloat16 [16384, 4096], P('blk', 'hid'), may hold values from -6 to 6
- coarse_weight: bfloat16 [4096, 4096], P('hid', 'blk'), may hold values from -0.25 to 0.25
- fine_weight: bfloat16 [512, 4096, 256], P('blk', 'hid'), may hold values from -0.25 to 0.25
- block_cluster: int32 [512], replicated, may hold values from 0 to 4095
- routes: int32 [16384, 8], P('blk'), may hold values from 0 to 511, as said below
- target_route: int32 [16384], P('blk'), may hold values from 0 to 7
- target_offset: int32 [16384], P('blk'), may hold values from 0 to 255
Outputs:
- row_loss: float32 [16384], P('blk')
- block_prob: float32 [16384, 8], P('blk')
Inputs may be any that keep to these rules, and one draw needn't show every extreme that they name: `routes`: each row lists 8 different blocks; among the 256 rows of one index of blk (aligned blocks of rows) no block is listed by more than 8 rows and some block is listed by exactly 8 of them; among those rows the 8 blocks of one index of blk are listed 48 times in all at the most, and exactly 48 times for some index.
All inputs are finite; a program needn't handle non-finite values.
Results may differ from a plain program's by a relative error of at most 0.0003.
Values may be sent and summed in bfloat16 or wider, within the bound.
No kernel may reach another device: no remote copies, remote signals or barrier semaphores. Data moves between devices by JAX's collectives and lax.ppermute only.
A program may use at most 128 MiB of HBM per device.

v0:
```python
import jax
import jax.numpy as jnp
from jax import lax
from jax.sharding import PartitionSpec as P


def pair_slots(route_rows, capacity):
    blocks_flat = route_rows.reshape(-1)
    count = blocks_flat.shape[0]
    sort_order = jnp.argsort(blocks_flat, stable=True)
    sorted_blocks = blocks_flat[sort_order]
    starts = jnp.searchsorted(sorted_blocks, sorted_blocks, side="left")
    rank_sorted = jnp.arange(count, dtype=jnp.int32) - starts
    rank_pairs = jnp.zeros((count,), jnp.int32).at[sort_order].set(rank_sorted)
    return blocks_flat * capacity + rank_pairs


def block_scores(logits, offsets):
    block_mass = jax.nn.logsumexp(logits, axis=-1)
    label_index = jnp.arange(logits.shape[-1], dtype=jnp.int32)
    target_value = jnp.sum(jnp.where(label_index == offsets[..., None], logits, 0.0), axis=-1)
    return (block_mass, target_value)


def build_send(features, pair_index, slot_count, route_width, extra_values, defaults):
    row_count = features.shape[0]
    pair_row = jnp.arange(row_count * route_width, dtype=jnp.int32) // route_width
    row_table = jnp.zeros((slot_count,), jnp.int32).at[pair_index].set(pair_row)
    filled = jnp.zeros((slot_count,), jnp.bool_).at[pair_index].set(True)
    send_rows = jnp.where(filled[:, None], features[row_table], jnp.zeros((), features.dtype))
    tables = tuple(
        (
            jnp.full((slot_count,), fill_value, jnp.int32).at[pair_index].set(values.reshape(-1))
            for values, fill_value in zip(extra_values, defaults)
        )
    )
    return (send_rows, tables)


def local(features, coarse_weight, fine_weight, block_cluster, routes, target_route, target_offset):
    row_count = features.shape[0]
    part_width = features.shape[1]
    blocks_dev = fine_weight.shape[0]
    label_count = fine_weight.shape[2]
    route_width = routes.shape[1]
    group_count = lax.axis_size("blk")
    block_total = blocks_dev * group_count
    capacity = 2 * row_count * route_width // block_total
    slot_width = blocks_dev * capacity
    partial_coarse = jnp.dot(
        features,
        lax.all_gather(coarse_weight, "blk", axis=1, tiled=True),
        preferred_element_type=jnp.float32,
    )
    route_cluster = block_cluster[routes]
    coarse = lax.psum(partial_coarse, "hid")
    coarse_lse = jax.nn.logsumexp(coarse, axis=1)
    coarse_pick = jnp.take_along_axis(coarse, route_cluster, axis=1) - coarse_lse[:, None]
    slot_index = pair_slots(routes, capacity)
    is_target = jnp.arange(route_width, dtype=jnp.int32)[None, :] == target_route[:, None]
    offset_grid = jnp.where(is_target, target_offset[:, None], -1)
    send_rows, tables = build_send(
        features, slot_index, block_total * capacity, route_width, (offset_grid,), (-1,)
    )
    send_offsets = tables[0]
    got_rows, got_offsets = (
        lax.all_to_all(
            send_rows.reshape(group_count, slot_width, part_width),
            "blk",
            split_axis=0,
            concat_axis=0,
            tiled=True,
        ),
        lax.all_to_all(
            send_offsets.reshape(group_count, slot_width),
            "blk",
            split_axis=0,
            concat_axis=0,
            tiled=True,
        ),
    )
    got_rows = got_rows.reshape(group_count, blocks_dev, capacity, part_width)
    slot_fine = jnp.einsum(
        "sbcd,bdl->sbcl", got_rows, fine_weight, preferred_element_type=jnp.float32
    )
    slot_fine = slot_fine.reshape(group_count, slot_width, label_count)
    fine_part = lax.psum_scatter(slot_fine, "hid", scatter_dimension=1, tiled=True)
    quarter = fine_part.shape[1]
    offset_part = lax.dynamic_slice_in_dim(got_offsets, lax.axis_index("hid") * quarter, quarter, 1)
    block_mass, target_value = block_scores(fine_part, offset_part)
    back_mass, back_target = (
        lax.all_to_all(block_mass, "blk", split_axis=0, concat_axis=0, tiled=True),
        lax.all_to_all(target_value, "blk", split_axis=0, concat_axis=0, tiled=True),
    )
    back_mass, back_target = (
        lax.all_gather(back_mass, "hid", axis=1, tiled=True),
        lax.all_gather(back_target, "hid", axis=1, tiled=True),
    )
    pair_mass = jnp.take(back_mass.reshape(-1), slot_index).reshape(row_count, route_width)
    target_logit = jnp.sum(
        jnp.take(back_target.reshape(-1), slot_index).reshape(row_count, route_width), axis=1
    )
    fine_lse = jax.nn.logsumexp(pair_mass, axis=1)
    log_prob = pair_mass - fine_lse[:, None]
    block_prob = jnp.exp(log_prob)
    row_loss = fine_lse - target_logit + jnp.sum(block_prob * (log_prob - coarse_pick), axis=1)
    return (row_loss, block_prob)


def solution(mesh):
    placed = (
        P("blk", "hid"),
        P("hid", "blk"),
        P("blk", "hid", None),
        P(),
        P("blk", None),
        P("blk"),
        P("blk"),
    )
    return jax.shard_map(
        local, mesh=mesh, in_specs=placed, out_specs=(P("blk"), P("blk", None)), check_vma=False
    )
```

profile of v0, /device:TPU:1, one launch (start us, length us, event | category | flops | bytes accessed | tf_op | source)
XLA Modules:
  0.0 580.7 jit_solution(12170328258044067903)
XLA Ops:
  7.2 0.7 all-gather.4.cloned.1.call-update
  7.9 0.8 copy.42
  8.8 0.1 reshape.129
  8.9 5.0 sort.17
  13.9 11.8 %gather_fusion.1 = s32[2048]{0:T(1024)S(1)} fusion(s32[2048]{0:T(1024)S(1)} %reshape.129, s32[2048]{0:T(1024)S(1)} %get-tuple-element.112), kind=kCustom, calls=%fused_computation.3 | custom fusion | bytes 24576 | tf_op jit(solution)/shard_map/gather | solution.py:11
  25.7 142.4 %while.25 = (s32[]{:T(128)}, u32[2048]{0:T(1024)S(1)}, u32[2048]{0:T(1024)S(1)}, s32[2048]{0:T(1024)S(1)}, s32[]{:T(128)}, /*index=5*/s32[]{:T(128)}, s32[]{}) while((s32[]{:T(128)}, u32[2048]{0:T(1024)S(1)}, u32[2048]{0:T(1024)S(1)}, s32[2048]{0:T(1024)S(1)}, s32[]{:T(128)}, /*index=5*/s32[]{:T(128)}, s32[]{}) %tuple.50), condition=%wide.region_2.0_spmd.clone, body=%wide.region_1.0_spmd.clone.sunk | while | flops 38916 | bytes 135269 | solution.py:12
  25.7 11.8 %gather_fusion = s32[2048]{0:T(1024)S(1)} fusion(s32[2048]{0:T(1024)S(1)} %get-tuple-element.161, u32[2048]{0:T(1024)S(1)} %broadcast_clamp_fusion.5), kind=kCustom, calls=%fused_computation.clone.clone.1 | custom fusion | bytes 24576 | tf_op jit(solution)/shard_map/jit(searchsorted)/jit(_searchsorted_scan_impl)/vmap(jit(_searchsorted_scan_impl))/while/body/eval_jaxpr/gather | solution.py:12
  37.6 11.8 %gather_fusion = s32[2048]{0:T(1024)S(1)} fusion(s32[2048]{0:T(1024)S(1)} %get-tuple-element.161, u32[2048]{0:T(1024)S(1)} %broadcast_clamp_fusion.5), kind=kCustom, calls=%fused_computation.clone.clone.1 | custom fusion | bytes 24576 | tf_op jit(solution)/shard_map/jit(searchsorted)/jit(_searchsorted_scan_impl)/vmap(jit(_searchsorted_scan_impl))/while/body/eval_jaxpr/gather | solution.py:12
  49.5 11.8 %gather_fusion = s32[2048]{0:T(1024)S(1)} fusion(s32[2048]{0:T(1024)S(1)} %get-tuple-element.161, u32[2048]{0:T(1024)S(1)} %broadcast_clamp_fusion.5), kind=kCustom, calls=%fused_computation.clone.clone.1 | custom fusion | bytes 24576 | tf_op jit(solution)/shard_map/jit(searchsorted)/jit(_searchsorted_scan_impl)/vmap(jit(_searchsorted_scan_impl))/while/body/eval_jaxpr/gather | solution.py:12
  61.3 11.8 %gather_fusion = s32[2048]{0:T(1024)S(1)} fusion(s32[2048]{0:T(1024)S(1)} %get-tuple-element.161, u32[2048]{0:T(1024)S(1)} %broadcast_clamp_fusion.5), kind=kCustom, calls=%fused_computation.clone.clone.1 | custom fusion | bytes 24576 | tf_op jit(solution)/shard_map/jit(searchsorted)/jit(_searchsorted_scan_impl)/vmap(jit(_searchsorted_scan_impl))/while/body/eval_jaxpr/gather | solution.py:12
  73.2 11.8 %gather_fusion = s32[2048]{0:T(1024)S(1)} fusion(s32[2048]{0:T(1024)S(1)} %get-tuple-element.161, u32[2048]{0:T(1024)S(1)} %broadcast_clamp_fusion.5), kind=kCustom, calls=%fused_computation.clone.clone.1 | custom fusion | bytes 24576 | tf_op jit(solution)/shard_map/jit(searchsorted)/jit(_searchsorted_scan_impl)/vmap(jit(_searchsorted_scan_impl))/while/body/eval_jaxpr/gather | solution.py:12
  85.1 11.8 %gather_fusion = s32[2048]{0:T(1024)S(1)} fusion(s32[2048]{0:T(1024)S(1)} %get-tuple-element.161, u32[2048]{0:T(1024)S(1)} %broadcast_clamp_fusion.5), kind=kCustom, calls=%fused_computation.clone.clone.1 | custom fusion | bytes 24576 | tf_op jit(solution)/shard_map/jit(searchsorted)/jit(_searchsorted_scan_impl)/vmap(jit(_searchsorted_scan_impl))/while/body/eval_jaxpr/gather | solution.py:12
  96.9 11.8 %gather_fusion = s32[2048]{0:T(1024)S(1)} fusion(s32[2048]{0:T(1024)S(1)} %get-tuple-element.161, u32[2048]{0:T(1024)S(1)} %broadcast_clamp_fusion.5), kind=kCustom, calls=%fused_computation.clone.clone.1 | custom fusion | bytes 24576 | tf_op jit(solution)/shard_map/jit(searchsorted)/jit(_searchsorted_scan_impl)/vmap(jit(_searchsorted_scan_impl))/while/body/eval_jaxpr/gather | solution.py:12
  108.8 11.8 %gather_fusion = s32[2048]{0:T(1024)S(1)} fusion(s32[2048]{0:T(1024)S(1)} %get-tuple-element.161, u32[2048]{0:T(1024)S(1)} %broadcast_clamp_fusion.5), kind=kCustom, calls=%fused_computation.clone.clone.1 | custom fusion | bytes 24576 | tf_op jit(solution)/shard_map/jit(searchsorted)/jit(_searchsorted_scan_impl)/vmap(jit(_searchsorted_scan_impl))/while/body/eval_jaxpr/gather | solution.py:12
  120.7 11.8 %gather_fusion = s32[2048]{0:T(1024)S(1)} fusion(s32[2048]{0:T(1024)S(1)} %get-tuple-element.161, u32[2048]{0:T(1024)S(1)} %broadcast_clamp_fusion.5), kind=kCustom, calls=%fused_computation.clone.clone.1 | custom fusion | bytes 24576 | tf_op jit(solution)/shard_map/jit(searchsorted)/jit(_searchsorted_scan_impl)/vmap(jit(_searchsorted_scan_impl))/while/body/eval_jaxpr/gather | solution.py:12
  132.5 11.8 %gather_fusion = s32[2048]{0:T(1024)S(1)} fusion(s32[2048]{0:T(1024)S(1)} %get-tuple-element.161, u32[2048]{0:T(1024)S(1)} %broadcast_clamp_fusion.5), kind=kCustom, calls=%fused_computation.clone.clone.1 | custom fusion | bytes 24576 | tf_op jit(solution)/shard_map/jit(searchsorted)/jit(_searchsorted_scan_impl)/vmap(jit(_searchsorted_scan_impl))/while/body/eval_jaxpr/gather | solution.py:12
  144.4 11.8 %gather_fusion = s32[2048]{0:T(1024)S(1)} fusion(s32[2048]{0:T(1024)S(1)} %get-tuple-element.161, u32[2048]{0:T(1024)S(1)} %broadcast_clamp_fusion.5), kind=kCustom, calls=%fused_computation.clone.clone.1 | custom fusion | bytes 24576 | tf_op jit(solution)/shard_map/jit(searchsorted)/jit(_searchsorted_scan_impl)/vmap(jit(_searchsorted_scan_impl))/while/body/eval_jaxpr/gather | solution.py:12
  156.3 11.8 %gather_fusion = s32[2048]{0:T(1024)S(1)} fusion(s32[2048]{0:T(1024)S(1)} %get-tuple-element.161, u32[2048]{0:T(1024)S(1)} %broadcast_clamp_fusion.5), kind=kCustom, calls=%fused_computation.clone.clone.1 | custom fusion | bytes 24576 | tf_op jit(solution)/shard_map/jit(searchsorted)/jit(_searchsorted_scan_impl)/vmap(jit(_searchsorted_scan_impl))/while/body/eval_jaxpr/gather | solution.py:12
  168.1 8.0 %scatter_custom_fusion = s32[2048]{0:T(1024)S(1)} fusion(s32[2048]{0:T(1024)S(1)} %get-tuple-element.113, s32[2048]{0:T(1024)S(1)} %convert_subtract_fusion, s32[]{:T(128)} %constant.95.clone.1), kind=kCustom, calls=%fused_computation.64 | custom fusion | bytes 8196 | tf_op jit(solution)/shard_map/scatter | solution.py:14
  176.2 8.1 %scatter_custom_fusion.2 = s32[4096]{0:T(1024)S(1)} fusion(s32[2048]{0:T(1024)S(1)} %get-tuple-element.111, s32[2048]{0:T(1024)S(1)} %get-tuple-element.114, s32[]{:T(128)} %constant.95.clone.1), kind=kCustom, calls=%fused_computation.51 | custom fusion | bytes 16388 | tf_op jit(solution)/shard_map/scatter | solution.py:28
  184.3 9.1 %scatter_custom_fusion.1 = pred[4096]{0:T(1024)(128)(4,1)S(1)} fusion(s32[2048]{0:T(1024)S(1)} %get-tuple-element.111, pred[2048]{0:T(1024)(128)(4,1)S(1)} %broadcast.104, pred[]{:T(512)} %constant.93.clone.1), kind=kCustom, calls=%fused_computation.56 | custom fusion | bytes 4097 | tf_op jit(solution)/shard_map/scatter | solution.py:29
  193.4 0.1 broadcast_in_dim.103
  193.5 18.3 %gather_fusion.2 = bf16[4096,1024]{1,0:T(8,128)(2,1)} fusion(bf16[256,1024]{1,0:T(8,128)(2,1)S(1)} %copy-done, s32[4096]{0:T(1024)S(1)} %fusion.13), kind=kCustom, calls=%fused_computation.4 | custom fusion | bytes 16793600 | tf_op jit(solution)/shard_map/gather | solution.py:30
  211.8 7.2 %broadcast_select_fusion = bf16[64,64,1024]{2,1,0:T(8,128)(2,1)} fusion(bf16[64,64,1024]{2,1,0:T(8,128)(2,1)} %bitcast.29, pred[64,64]{1,0:T(8,128)(4,1)S(1)} %broadcast_in_dim.103), kind=kLoop, calls=%fused_computation.17 | loop fusion | flops 4194304 | bytes 16781312 | tf_op jit(solution)/shard_map/jit(_where)/select_n | solution.py:30
  219.0 13.2 %all-to-all-start = ((bf16[64,64,1024]{2,1,0:T(8,128)(2,1)}), bf16[64,64,1024]{2,1,0:T(8,128)(2,1)}, u32[]{:S(2)}, u32[]{:S(2)}) async-start(bf16[64,64,1024]{2,1,0:T(8,128)(2,1)} %broadcast_select_fusion), calls=%async_computation | async-start | bytes 16777216 | tf_op jit(solution)/shard_map/all_to_all | solution.py:67
  232.2 0.2 all-reduce.2.cloned.1.call-start
  232.4 7.7 %fusion.25 = f32[256,4096]{1,0:T(8,128)} fusion(bf16[256,1024]{1,0:T(8,128)(2,1)S(1)} %copy-done, bf16[1024,4096]{0,1:T(8,128)(2,1)} %all-gather.4.cloned.1.call-done), kind=kOutput, calls=%fused_computation.72 | convolution fusion | flops 2147483648 | bytes 13107200 | tf_op jit(solution)/shard_map/dot_general | solution.py:50
  240.2 177.7 %all-to-all-done = bf16[64,64,1024]{2,1,0:T(8,128)(2,1)} async-done(((bf16[64,64,1024]{2,1,0:T(8,128)(2,1)}), bf16[64,64,1024]{2,1,0:T(8,128)(2,1)}, u32[]{:S(2)}, u32[]{:S(2)}) %all-to-all-start) | async-done | bytes 8388640 | tf_op jit(solution)/shard_map/all_to_all | solution.py:67
  418.0 6.9 %fusion.3 = f32[64,8,8,256]{3,2,0,1:T(8,128)S(1)} fusion(bf16[8,1024,256]{2,1,0:T(8,128)(2,1)} %param.13, bf16[64,64,1024]{2,1,0:T(8,128)(2,1)} %all-to-all-done), kind=kOutput, calls=%fused_computation.21 | convolution fusion | flops 2147483648 | bytes 16777216 | tf_op jit(solution)/shard_map/sbcd,bdl->sbcl/dot_general | solution.py:83
  424.9 2.6 copy.61
  427.5 0.1 fusion.11
  427.7 0.1 reshape.218
  427.8 8.1 %scatter_custom_fusion.3 = s32[4096]{0:T(1024)S(1)} fusion(s32[2048]{0:T(1024)S(1)} %get-tuple-element.111, s32[2048]{0:T(1024)S(1)} %reshape.218, s32[]{:T(128)} %constant.104.clone.1), kind=kCustom, calls=%fused_computation.49 | custom fusion | bytes 16388 | tf_op jit(solution)/shard_map/scatter | solution.py:33
  435.9 0.7 all_to_all.26
  436.6 5.9 %all-to-all-start.2 = ((s32[64,1,64]{2,1,0:T(1,128)}), s32[64,1,64]{2,1,0:T(1,128)S(1)}, u32[]{:S(2)}, u32[]{:S(2)}) async-start(s32[64,1,64]{2,1,0:T(1,128)} %all_to_all.26), calls=%async_computation.3 | async-start | bytes 65536 | tf_op jit(solution)/shard_map/all_to_all | solution.py:74
  442.5 0.1 copy.50
  442.6 0.1 reshape.178
  442.7 13.2 %gather_fusion.3 = s32[2048]{0:T(1024)S(1)} fusion(s32[512]{0:T(512)S(1)} %copy-done.1, s32[2048]{0:T(1024)S(1)} %broadcast_clamp_fusion.1), kind=kCustom, calls=%fused_computation.5 | custom fusion | bytes 24576 | tf_op jit(solution)/shard_map/gather | solution.py:55
  456.0 0.1 gather.31
  456.1 0.1 reshape.177
  456.2 0.1 reshape.184
  456.4 0.1 constant_dynamic-slice_fusion
  456.6 2.5 reduce_max.32
  459.1 14.7 %reduce-scatter.2.cloned.1.call-done = f32[64,16,256]{2,1,0:T(8,128)} async-done(((f32[64,64,256]{2,1,0:T(8,128)}), f32[64,16,256]{2,1,0:T(8,128)}) %reduce-scatter.2.cloned.1.call-update) | async-done | bytes 1048592 | tf_op jit(solution)/shard_map/reduce_scatter | solution.py:87
  473.8 1.4 reduce_max.29
  475.3 2.5 select_reduce_fusion
  477.8 0.7 fusion.12
  478.4 10.6 %all-to-all-start.1 = ((f32[64,1,16]{2,1,0:T(1,128)}), f32[64,1,16]{2,1,0:T(1,128)S(1)}, u32[]{:S(2)}, u32[]{:S(2)}) async-start(f32[64,1,16]{2,1,0:T(1,128)} %fusion.12), calls=%async_computation.2 | async-start | bytes 65536 | tf_op jit(solution)/shard_map/all_to_all | solution.py:92
  489.0 2.9 exponential_reduce_fusion
  491.9 6.4 %all-to-all-done.1 = f32[64,1,16]{2,1,0:T(1,128)S(1)} async-done(((f32[64,1,16]{2,1,0:T(1,128)}), f32[64,1,16]{2,1,0:T(1,128)S(1)}, u32[]{:S(2)}, u32[]{:S(2)}) %all-to-all-start.1) | async-done | bytes 4128 | tf_op jit(solution)/shard_map/all_to_all | solution.py:92
  498.3 4.6 all-to-all-start.3
  503.0 27.0 %gather_fusion.4 = f32[2048]{0:T(1024)S(1)} fusion(f32[256,4096]{1,0:T(8,128)} %all-reduce.2.cloned.1.call-done, s32[2048]{0:T(1024)S(1)} %reshape.184), kind=kCustom, calls=%fused_computation.6 | custom fusion | bytes 32768 | tf_op jit(solution)/shard_map/jit(take_along_axis)/gather | solution.py:58
  530.0 0.1 reshape.187
  530.3 9.0 %all-gather = f32[64,1,64]{0,1,2:T(1,128)S(1)} all-gather(f32[64,1,16]{0,1,2:T(1,128)S(1)} %copy.45), channel_id=2, replica_groups=mesh['hid'=4,'blk'=64] {'hid'}, dimensions={2}, use_global_device_ids=true | all-gather | bytes 20480 | tf_op jit(solution)/shard_map/all_gather | solution.py:96
  539.5 9.0 %all-gather.1 = f32[64,1,64]{0,1,2:T(1,128)S(1)} all-gather(f32[64,1,16]{0,1,2:T(1,128)S(1)} %copy.47), channel_id=3, replica_groups=mesh['hid'=4,'blk'=64] {'hid'}, dimensions={2}, use_global_device_ids=true | all-gather | bytes 20480 | tf_op jit(solution)/shard_map/all_gather | solution.py:97
  548.7 11.8 %gather_fusion.5 = f32[2048]{0:T(1024)S(1)} fusion(f32[4096]{0:T(1024)S(1)} %reshape.132, s32[2048]{0:T(1024)S(1)} %get-tuple-element.110), kind=kCustom, calls=%fused_computation.1.clone | custom fusion | bytes 24576 | tf_op jit(solution)/shard_map/jit(_take)/gather | solution.py:99
  560.5 11.8 %gather_fusion.6 = f32[2048]{0:T(1024)S(1)} fusion(f32[4096]{0:T(1024)S(1)} %reshape.134, s32[2048]{0:T(1024)S(1)} %get-tuple-element.110), kind=kCustom, calls=%fused_computation.2.clone | custom fusion | bytes 24576 | tf_op jit(solution)/shard_map/jit(_take)/gather | solution.py:101
  572.3 0.1 reshape.133
  572.4 0.1 reduce_max.31
  572.6 0.2 exponential_reduce_fusion.2
  572.8 0.1 reshape.135
  572.9 0.1 reduce_sum.57
  573.0 0.6 multiply_reduce_fusion
  573.6 0.6 subtract_add_fusion
  (94 shorter events, 1.3 us)
Async XLA Ops:
  7.2 186.4 %copy-start = (bf16[256,1024]{1,0:T(8,128)(2,1)S(1)}, bf16[256,1024]{1,0:T(8,128)(2,1)}, u32[]{:S(2)}) copy-start(bf16[256,1024]{1,0:T(8,128)(2,1)} %param.11) | copy-start | bytes 1572868
  7.2 225.3 %all-gather.4.cloned.1.call-start = ((), (), s32[]{:S(2)}) async-start(), calls=%async_computation.6 | async-start | bytes 8519680 | tf_op jit(solution)/shard_map/all_gather | solution.py:52
  219.0 199.0 %all-to-all-start = ((bf16[64,64,1024]{2,1,0:T(8,128)(2,1)}), bf16[64,64,1024]{2,1,0:T(8,128)(2,1)}, u32[]{:S(2)}, u32[]{:S(2)}) async-start(bf16[64,64,1024]{2,1,0:T(8,128)(2,1)} %broadcast_select_fusion), calls=%async_computation | async-start | bytes 16777216 | tf_op jit(solution)/shard_map/all_to_all | solution.py:67
  232.2 224.4 %all-reduce.2.cloned.1.call-start = ((), (), s32[]{:S(2)}) async-start(), calls=%async_computation.7 | async-start | bytes 8388608 | tf_op jit(solution)/shard_map/psum | solution.py:56
  240.2 233.6 %reduce-scatter.2.cloned.1.call-start = ((), (), s32[]{:S(2)}) async-start(), calls=%async_computation.5 | async-start | bytes 5242880 | tf_op jit(solution)/shard_map/reduce_scatter | solution.py:87
  424.9 2.7 copy-start.3
  424.9 2.7 copy-start.4
  424.9 17.6 %copy-start.2 = (s32[256,8]{0,1:T(8,128)S(1)}, s32[256,8]{0,1:T(8,128)}, u32[]{:S(2)}) copy-start(s32[256,8]{0,1:T(8,128)} %param.15) | copy-start | bytes 24580
  424.9 17.8 %copy-start.1 = (s32[512]{0:T(512)S(1)}, s32[512]{0:T(512)}, u32[]{:S(2)}) copy-start(s32[512]{0:T(512)} %param.14) | copy-start | bytes 6148
  436.6 19.8 %all-to-all-start.2 = ((s32[64,1,64]{2,1,0:T(1,128)}), s32[64,1,64]{2,1,0:T(1,128)S(1)}, u32[]{:S(2)}, u32[]{:S(2)}) async-start(s32[64,1,64]{2,1,0:T(1,128)} %all_to_all.26), calls=%async_computation.3 | async-start | bytes 65536 | tf_op jit(solution)/shard_map/all_to_all | solution.py:74
  478.4 19.9 %all-to-all-start.1 = ((f32[64,1,16]{2,1,0:T(1,128)}), f32[64,1,16]{2,1,0:T(1,128)S(1)}, u32[]{:S(2)}, u32[]{:S(2)}) async-start(f32[64,1,16]{2,1,0:T(1,128)} %fusion.12), calls=%async_computation.2 | async-start | bytes 65536 | tf_op jit(solution)/shard_map/all_to_all | solution.py:92
  498.3 41.1 %all-to-all-start.3 = ((f32[64,1,16]{2,1,0:T(1,128)}), f32[64,1,16]{2,1,0:T(1,128)S(1)}, u32[]{:S(2)}, u32[]{:S(2)}) async-start(f32[64,1,16]{2,1,0:T(1,128)} %bitcast.9), calls=%async_computation.4 | async-start | bytes 65536 | tf_op jit(solution)/shard_map/all_to_all | solution.py:93
Sparse Core Ops, SparseCore 0:
  10.8 87.2 all-gather.3
  240.3 99.0 all-reduce.1
  427.6 46.1 reduce-scatter.1
where the time goes:
time: 587 us; the launch traced here: 581 us
  local copies, waits for them, and re-layouts  275 us (47%)
  waiting for transfers between devices  200 us (34%)
  starting transfers between devices  34.6 us (6%)
  other arithmetic  24.4 us (4%)
  blocking collectives  18.1 us (3%)
  matrix products  14.6 us (2%)
  between operations  14.2 us (2%)
    all_to_all x1, waiting for transfers between devices, local(): lax.all_to_all(send_rows.reshape(group_count, slot_width, part_width), 'b...  178 us
    gather x12, local copies, waits for them, and re-layouts, pair_slots(): starts = jnp.searchsorted(sorted_blocks, sorted_blocks, side='left')  141 us
    gather x4, local copies, waits for them, and re-layouts, local(): jnp.take_along_axis(coarse, route_cluster, axis=1) - coarse_lse[:, None]  27.3 us
    gather x1, local copies, waits for them, and re-layouts, build_send(): features[row_table]  18.3 us
    reduce_scatter x1, waiting for transfers between devices, local(): lax.psum_scatter(slot_fine, 'hid', scatter_dimension=1, tiled=True)  14.7 us
    gather x4, local copies, waits for them, and re-layouts, local(): route_cluster = block_cluster[routes]  13.5 us
    all_to_all x1, starting transfers between devices, local(): lax.all_to_all(send_rows.reshape(group_count, slot_width, part_width), 'b...  13.2 us
    gather x1, local copies, waits for them, and re-layouts, local(): jnp.take(back_mass.reshape(-1), slot_index).reshape(row_count, route_width)  11.8 us
  transfers between devices with their start and end apart: 7, of which 3 were waited for; matrix products, arithmetic and copies ran while one was open for 49% of the time, Pallas kernels for 0%

commit v1 on v0

v1 whole, which is shorter than its diff:
```python
import jax
import jax.numpy as jnp
from jax import lax
from jax.experimental import pallas as pl
from jax.experimental.pallas import tpu as pltpu
from jax.sharding import Mesh, PartitionSpec as P

F32 = jnp.float32
BF16 = jnp.bfloat16
I32 = jnp.int32

HID, NX, NZ, NC = 4, 4, 8, 2
ROWS = 256
PART = 1024
TOP = 8
BLK = 8
QB = NC * BLK
CAP = 8
LBL = 256
INFO = 16
SLOTS = 48
TIERS = SLOTS // CAP
PAIR = 2 * CAP
WIDE = 2 * ROWS
AWAY = ((0, 1, -1, 2), (-2, 3, -3, 4))
FOUR = 2 * PAIR
ARRIVE = {0: range(0, 2), 2: range(2, BLK), BLK: range(BLK, QB)}
GROUPS = NC * NX
EXT = ROWS + INFO
VMEM = 56 * 1024 * 1024


def iota(shape, dim):
    return lax.broadcasted_iota(I32, shape, dim)


def dot(a, b):
    return jnp.dot(a, b, preferred_element_type=F32)


def strict_upper():
    return jnp.where(iota((ROWS, ROWS), 0) < iota((ROWS, ROWS), 1), 1.0, 0.0).astype(BF16)


def other(core, half):
    return core + half - 2 * core * half


def pack_kernel(f_ref, routes_ref, place_ref, offset_ref, cluster_ref, out_ref):
    out_ref[0:ROWS, :] = f_ref[...]
    routes = routes_ref[...]
    clusters = cluster_ref[...]
    count = clusters.shape[1]
    table = jnp.concatenate([clusters >> 6, clusters & 63, jnp.zeros((14, count), I32)], axis=0)
    table = table.astype(F32).astype(BF16)
    groups, columns = [], []
    blocks = iota((count, ROWS), 0)
    for k in range(TOP):
        hot = jnp.where(blocks == routes[k : k + 1, :], 1.0, 0.0).astype(BF16)
        found = dot(table, hot)
        groups.append(found[0:1, :])
        columns.append(found[1:2, :])
    places = [place_ref[...].astype(F32), offset_ref[...].astype(F32), jnp.zeros((6, ROWS), F32)]
    left = jnp.concatenate([(routes - 256).astype(F32)] + columns, axis=0)
    right = jnp.concatenate(groups + places, axis=0)
    rest = jnp.zeros((INFO, PART - WIDE), F32)
    out_ref[ROWS:EXT, :] = jnp.concatenate([left, right, rest], axis=1).astype(BF16)


def select_more_kernel(at_ref, a_ref, b_ref, begun_ref, rows_ref):
    select_kernel(at_ref, a_ref, b_ref, rows_ref)


def select_kernel(at_ref, a_ref, b_ref, rows_ref):
    z, core = at_ref[1], at_ref[2]
    count = GROUPS * BLK
    index = iota((count, ROWS), 0)
    device = ((index >> 3) & 3) * (NZ * NC) + z * NC + other(core, index >> 5)
    blocks = device * BLK + (index & 7)
    upper = strict_upper()
    ones = jnp.ones((ROWS, ROWS), BF16)
    row, col = iota((count, count), 0), iota((count, count), 1)
    before = jnp.where(((row >> 3) == (col >> 3)) & (col < row), 1.0, 0.0).astype(BF16)
    slot_of = iota((SLOTS, ROWS), 0).astype(F32)
    eye = iota((SLOTS, 128), 0) == iota((SLOTS, 128), 1)

    def as_line(column):
        return jnp.sum(jnp.where(eye, column, 0.0), axis=0, keepdims=True)

    picked, owners, places = [], [], []
    for g_ref in (a_ref, b_ref):
        info = g_ref[ROWS:EXT, 0:WIDE].astype(F32)
        routes = info[0:TOP, 0:ROWS].astype(I32) + 256
        place = info[TOP : TOP + 1, ROWS:].astype(I32)
        offset = info[TOP + 1 : TOP + 2, ROWS:]
        hit = jnp.zeros((count, ROWS), F32)
        target = jnp.zeros((1, ROWS), I32)
        for k in range(TOP):
            hit = jnp.where(routes[k : k + 1, :] == blocks, 1.0, hit)
            target = jnp.where(place == k, routes[k : k + 1, :], target)
        held = hit.astype(BF16)
        start = dot(before, dot(held, ones).astype(BF16))
        slot = jnp.where(hit > 0.5, dot(held, upper) + start, -1.0)
        wanted = jnp.where(blocks == target, slot, -1.0)
        hots = []
        for g in range(GROUPS):
            label = jnp.full((SLOTS, ROWS), -1.0, F32)
            for b in range(BLK):
                label = jnp.where(slot[g * BLK + b : g * BLK + b + 1, :] == slot_of, float(b), label)
            hots.append(jnp.where(label > -0.5, 1.0, 0.0).astype(BF16))
            owners.append(as_line(jnp.max(label, axis=1, keepdims=True)))
            mine = jnp.max(wanted[g * BLK : (g + 1) * BLK, :], axis=0, keepdims=True)
            places.append(
                as_line(
                    jnp.sum(jnp.where(mine == slot_of, offset + 1.0, 0.0), axis=1, keepdims=True)
                )
            )
        hots = jnp.concatenate(hots, axis=0)
        picked.append(dot(hots, g_ref[0:ROWS, :]).reshape(GROUPS, TIERS, CAP, PART))
    both = jnp.concatenate(picked, axis=2).astype(BF16)
    for g in range(GROUPS):
        rows_ref[g % NX, (g // NX) * TIERS : (g // NX + 1) * TIERS] = both[g]
    for d in range(NX):
        lines = []
        for half in range(NC):
            g = half * NX + d
            lines += [owners[g], owners[GROUPS + g], places[g], places[GROUPS + g]]
        lines = jnp.concatenate(lines + [jnp.zeros((8, 128), F32)], axis=0)
        lines = jnp.concatenate([lines, jnp.zeros((PAIR, PART - 128), F32)], axis=1)
        rows_ref[d, NC * TIERS] = lines.astype(BF16)


def partial_kernel(a_ref, b_ref, c_ref, d_ref, w_ref, out_ref):
    for s, ref in enumerate((a_ref, b_ref, c_ref, d_ref)):
        out_ref[:, s * ROWS : (s + 1) * ROWS] = lax.dot_general(
            w_ref[...], ref[0:ROWS, :], (((1,), (1,)), ((), ())), preferred_element_type=F32
        )


def slot_lines(meta, half, kind):
    eye = iota((SLOTS, 128), 0) == iota((SLOTS, 128), 1)
    columns = []
    for s in range(4):
        at = (s // 2) * PAIR + half * 4 + kind * 2 + s % 2
        column = jnp.sum(jnp.where(eye, meta[at : at + 1, :], 0.0), axis=1, keepdims=True)
        columns.append(jnp.broadcast_to(column, (SLOTS, LBL)))
    return jnp.concatenate(
        [c[t * CAP : (t + 1) * CAP, :] for t in range(TIERS) for c in columns], axis=0
    )


def fine_kernel(own_ref, peer_ref, r_ref, out_ref, held_ref, owner_ref, sems):
    copies = []
    for i in range(QB):
        source = own_ref if i < BLK else peer_ref
        copies.append(pltpu.make_async_copy(source.at[i % BLK], held_ref.at[i], sems.at[i]))
        copies[i].start()
    for half in range(NC):
        for x in range(NX):
            meta = r_ref[x, NC * TIERS, :, 0:128].astype(F32)
            owner_ref[x] = slot_lines(meta, half, 0).reshape(TIERS, FOUR, LBL)
        for b in range(BLK):
            for i in ARRIVE.get(half * BLK + b, ()):
                copies[i].wait()
            end = min(b + 1, TIERS)
            rows = r_ref[:, half * TIERS : half * TIERS + end].reshape(NX * end * FOUR, PART)
            part = dot(rows, held_ref[half * BLK + b])
            for x in range(NX):
                for t in range(end):
                    at = (x * end + t) * FOUR
                    piece = part[at : at + FOUR]
                    if t < b:
                        piece = jnp.where(owner_ref[x, t] == float(b), piece, out_ref[x, half, t])
                    out_ref[x, half, t] = piece


def score(y, h, meta_ref):
    rows = NC * TIERS * FOUR
    y = y.reshape(rows, LBL)
    meta = meta_ref[h, 0, :, 0:128].astype(F32)
    wanted = jnp.concatenate([slot_lines(meta, half, 1) for half in range(NC)], axis=0)
    label = iota((rows, LBL), 1).astype(F32) + 1.0
    top = jnp.max(y, axis=1, keepdims=True)
    mass = top + jnp.log(jnp.sum(jnp.exp(y - top), axis=1, keepdims=True))
    target = jnp.sum(jnp.where(label == wanted, y, 0.0), axis=1, keepdims=True)
    order = iota((rows, LBL), 0)
    tier = order // FOUR
    half = jnp.where(tier >= TIERS, 1, 0)
    slot = half * 128 + (tier - half * TIERS) * CAP + (order & 7)
    lane = iota((rows, LBL), 1)
    packed = jnp.where(lane == slot, mass, 0.0) + jnp.where(lane == slot + 64, target, 0.0)
    packed = jnp.sum(packed.reshape(NC * TIERS, 4, CAP, LBL), axis=2)
    return jnp.sum(packed, axis=0)


def score_kernel(at_ref, y_ref, meta_ref, out_ref):
    out_ref[0:4, :] = score(y_ref[0], at_ref[3], meta_ref)
    out_ref[4:8, :] = jnp.zeros((4, LBL), F32)


def score_last_kernel(at_ref, y_ref, meta_ref, first_ref, out_ref):
    z, core, h = at_ref[1], at_ref[2], at_ref[3]
    y = y_ref[0] + y_ref[1] + y_ref[2] + y_ref[3]
    last = score(y, h, meta_ref)
    out_ref[...] = jnp.zeros_like(out_ref)
    for i, lines in enumerate((first_ref, last)):
        for s in range(4):
            to = (z + NZ + AWAY[i][s]) & (NZ - 1)
            for d in range(HID):
                at = (((d * NX + h) * NZ + to) * NC + core) * NC
                for half in range(NC):
                    line = lines[s : s + 1, half * 128 : (half + 1) * 128]
                    out_ref[pl.ds(at + half, 1), :] = line


def coarse_lines(at_ref, c_ref, infos):
    z, h = at_ref[1], at_ref[3]
    width = c_ref.shape[0]
    column = iota((width, ROWS), 0)
    out = []
    for s, info_ref in enumerate(infos):
        logits = c_ref[:, s * ROWS : (s + 1) * ROWS]
        info = info_ref[...].astype(F32).astype(I32)
        inside = info[TOP : 2 * TOP, 0:ROWS]
        group = info[0:TOP, ROWS:WIDE]
        place = ((group >> 4) * NC + (group & 1)) * 64 + inside - h * width
        place = jnp.where(((group >> 1) & 7) == z, place, -1)
        top = jnp.max(logits, axis=0, keepdims=True)
        total = jnp.sum(jnp.exp(logits - top), axis=0, keepdims=True)
        lines = [top, total, jnp.zeros((6, ROWS), F32)]
        for k in range(TOP):
            lines.append(
                jnp.sum(
                    jnp.where(column == place[k : k + 1, :], logits, 0.0), axis=0, keepdims=True
                )
            )
        out.append(jnp.concatenate(lines, axis=0))
    return out


def coarse_kernel(at_ref, c_ref, i0, i1, i2, i3, out_ref):
    for s, lines in enumerate(coarse_lines(at_ref, c_ref, (i0, i1, i2, i3))):
        out_ref[s] = lines


def coarse_last_kernel(at_ref, c_ref, i0, i1, i2, i3, first_ref, out_ref):
    z = at_ref[1]
    last = coarse_lines(at_ref, c_ref, (i0, i1, i2, i3))
    away = [d for four in AWAY for d in four]
    for i in range(NZ):
        lines = first_ref[i] if i < NZ // 2 else last[i - NZ // 2]
        for d in range(HID):
            out_ref[d, (z + NZ + away[i]) & (NZ - 1)] = lines


def finish_kernel(at_ref, fine_ref, coarse_ref, routes_ref, loss_ref, prob_ref):
    x, core = at_ref[0], at_ref[2]
    routes = routes_ref[...]
    chips = NX * NZ
    index = iota((QB * chips, ROWS), 0)
    q = index >> 5
    block = ((index & 31) * NC + other(core, q >> 3)) * BLK + (q & 7)
    hit = jnp.zeros((QB * chips, ROWS), F32)
    for k in range(TOP):
        hit = jnp.where(routes[k : k + 1, :] == block, 1.0, hit)
    held = hit.astype(BF16)
    rank = dot(held, strict_upper())
    count = dot(held, jnp.ones((ROWS, ROWS), BF16))
    slots = []
    for half in range(NC):
        start = jnp.zeros((chips, ROWS), F32)
        for b in range(BLK):
            at = (half * BLK + b) * chips
            slots.append(rank[at : at + chips] + start)
            start = start + count[at : at + chips]
    slots = jnp.concatenate(slots, axis=0)

    table = fine_ref[pl.ds(x * (chips * NC * NC), chips * NC * NC), :]
    high = table.astype(BF16)
    rest = table - high.astype(F32)
    middle = rest.astype(BF16)
    low = (rest - middle.astype(F32)).astype(BF16)
    pieces = jnp.concatenate([high, middle, low], axis=0)
    row_of = iota((chips * NC * NC, ROWS), 0)
    lane_of = iota((128, ROWS), 0).astype(F32)
    pair = []
    target = jnp.zeros((1, ROWS), F32)
    for k in range(TOP):
        route = routes[k : k + 1, :]
        slot = jnp.sum(jnp.where(route == block, slots, 0.0), axis=0, keepdims=True)
        line = ((route >> 4) * NC + core) * NC + other(core, (route >> 3) & 1)
        hot = jnp.where(line == row_of, 1.0, 0.0).astype(BF16)
        found = lax.dot_general(
            pieces,
            jnp.concatenate([hot, hot, hot], axis=0),
            (((0,), (0,)), ((), ())),
            preferred_element_type=F32,
        )
        pair.append(jnp.sum(jnp.where(lane_of == slot, found, 0.0), axis=0, keepdims=True))
        target = target + jnp.sum(
            jnp.where(lane_of == slot + 64.0, found, 0.0), axis=0, keepdims=True
        )
    pair = jnp.concatenate(pair, axis=0)
    top = jnp.max(pair, axis=0, keepdims=True)
    fine_lse = top + jnp.log(jnp.sum(jnp.exp(pair - top), axis=0, keepdims=True))
    log_prob = pair - fine_lse
    prob = jnp.exp(log_prob)

    parts = coarse_ref[...]
    tops = parts[:, 0, :]
    peak = jnp.max(tops, axis=0, keepdims=True)
    total = jnp.sum(parts[:, 1, :] * jnp.exp(tops - peak), axis=0, keepdims=True)
    coarse_lse = peak + jnp.log(total)
    picked = jnp.sum(parts[:, 8:16, :], axis=0) - coarse_lse
    kl = jnp.sum(prob * (log_prob - picked), axis=0, keepdims=True)
    loss_ref[...] = fine_lse - target + kl
    prob_ref[...] = prob


def params(**more):
    return pltpu.CompilerParams(vmem_limit_bytes=VMEM, **more)


def smem():
    return pl.BlockSpec(memory_space=pltpu.SMEM)


def shape(dims, kind):
    return jax.ShapeDtypeStruct(dims, kind)


def swap(value, axes, split=0):
    return lax.all_to_all(value, axes, split, split, tiled=True)


def local(features, coarse_weight, fine_weight, block_cluster, routes, target_route, target_offset):
    ax = lax.axis_index
    at = jnp.stack([ax("x"), ax("z"), ax("c"), ax("hid")]).astype(I32)
    hbm = pl.BlockSpec(memory_space=pl.ANY)
    routes_t = routes.T

    full = lambda *dims: pl.BlockSpec(dims, lambda i: (0,) * len(dims))

    def run(kernel, specs, out, *operands, out_specs=None, scratch=(), **more):
        outs = out if isinstance(out, list) else [out]
        specs = [full(*o.shape) if spec is None else spec for spec, o in zip(specs, operands)]
        return pl.pallas_call(
            kernel,
            grid=(1,),
            in_specs=specs,
            out_specs=out_specs or [full(*o.shape) for o in outs],
            out_shape=outs,
            scratch_shapes=scratch,
            compiler_params=params(),
            **more,
        )(*operands)

    (here,) = run(
        pack_kernel,
        [None] * 5,
        shape((EXT, PART), BF16),
        features,
        routes_t,
        target_route[None],
        target_offset[None],
        block_cluster[None],
    )
    up = [(i, (i + 1) % NZ) for i in range(NZ)]
    down = [(i, (i - 1) % NZ) for i in range(NZ)]
    from_up, from_down = [here], [here]
    for step in range(NZ // 2):
        if step < NZ // 2 - 1:
            from_up.append(lax.ppermute(from_up[-1], "z", down))
        from_down.append(lax.ppermute(from_down[-1], "z", up))
    peer_weight = lax.ppermute(fine_weight, "c", [(0, 1), (1, 0)])
    coarse_t = lax.all_gather(coarse_weight.T, ("x", "c"), axis=0, tiled=True)
    columns = coarse_t.shape[0]

    near = (here, from_up[1], from_down[1], from_up[2])
    far = (from_down[2], from_up[3], from_down[3], from_down[4])
    tiers = NC * TIERS + 1
    last_run = [here]

    def in_turn(call, first, *more):
        first, _ = lax.optimization_barrier((first, last_run[0]))
        (last_run[0],) = call(first, *more)
        return last_run[0]

    def select(four, *waits):
        out = shape((NX, tiers, FOUR, PART), BF16)
        block = (NX, tiers, PAIR, PART)

        def begin(a, b):
            to = pl.BlockSpec(block, lambda i: (0, 0, 0, 0))
            return run(select_kernel, [smem(), None, None], out, at, a, b, out_specs=[to])

        def end(a, b, begun):
            to = pl.BlockSpec(block, lambda i: (0, 0, 1, 0))
            specs = [smem(), None, None, hbm]
            return run(
                select_more_kernel,
                specs,
                out,
                at,
                a,
                b,
                begun,
                out_specs=[to],
                input_output_aliases={3: 0},
            )

        first = lax.optimization_barrier((four[0], waits[0]))[0]
        begun = in_turn(begin, first, four[1])
        first = lax.optimization_barrier((four[2], waits[1]))[0]
        return swap(in_turn(end, first, four[3], begun), "x")

    def partial(four, *waits):
        def call(*four):
            out = shape((columns, NX * ROWS), F32)
            return run(partial_kernel, [None] * 5, out, *four, coarse_t)

        first = lax.optimization_barrier((four[0], *waits))[0]
        out = in_turn(call, first, *four[1:])
        return lax.psum_scatter(out, "hid", scatter_dimension=0, tiled=True)

    info = pl.BlockSpec((INFO, WIDE), lambda i: (ROWS // INFO, 0))

    def coarse(kernel, part, four, out, *more):
        def call(c):
            specs = [smem(), None] + [info] * 4 + [None] * len(more)
            return run(kernel, specs, out, at, c, *four, *more)

        return in_turn(call, part)

    def fine(rows):
        def call(rows):
            return run(
                fine_kernel,
                [hbm, hbm, None],
                shape((NX, NC, TIERS, FOUR, LBL), F32),
                fine_weight,
                peer_weight,
                rows,
                scratch=[
                    pltpu.VMEM((QB, PART, LBL), BF16),
                    pltpu.VMEM((NX, TIERS, FOUR, LBL), F32),
                    pltpu.SemaphoreType.DMA((QB,)),
                ],
                cost_estimate=pl.CostEstimate(
                    flops=8 * 10**9, bytes_accessed=40 * 2**20, transcendentals=0
                ),
            )

        return in_turn(call, rows)

    meta = pl.BlockSpec((NX, 1, FOUR, PART), lambda i: (0, NC * TIERS, 0, 0))

    def scored(kernel, fine, rows, out, *before):
        def call(fine):
            specs = [smem(), None, meta] + [None] * len(before)
            return run(kernel, specs, out, at, fine, rows, *before)

        return in_turn(call, fine)

    rows_near = select(near, from_down[1], from_down[2])
    part_near = partial(near)
    rows_far = select(far, from_down[3], from_down[4])
    part_far = partial(far, rows_near)
    fine_near = lax.psum_scatter(fine(rows_near), "hid", scatter_dimension=0, tiled=True)
    lines = coarse(coarse_kernel, part_near, near, shape((NZ // 2, 16, ROWS), F32))
    lines = coarse(coarse_last_kernel, part_far, far, shape((HID, NZ, 16, ROWS), F32), lines)
    lines = swap(lines.reshape(HID * NZ, 16, ROWS), ("hid", "z"))
    fine_far, lines = lax.optimization_barrier((fine(rows_far), lines))
    fine_far = swap(fine_far, "hid")
    first = scored(score_kernel, fine_near, rows_near, shape((8, LBL), F32))
    table = scored(
        score_last_kernel, fine_far, rows_far, shape((HID * NX * NZ * NC * NC, 128), F32), first
    )
    table = swap(table, ("hid", "x", "z", "c"))

    loss, prob = run(
        finish_kernel,
        [smem(), None, None, None],
        [shape((1, ROWS), F32), shape((TOP, ROWS), F32)],
        at,
        table,
        lines,
        routes_t,
    )
    return loss.reshape(ROWS), prob.T


def solution(mesh):
    fine_mesh = Mesh(mesh.devices.reshape(HID, NX, NZ, NC), ("hid", "x", "z", "c"))
    blk = ("x", "z", "c")
    placed = (P(blk, "hid"), P("hid", blk), P(blk, "hid", None), P(), P(blk, None), P(blk), P(blk))
    return jax.shard_map(
        local, mesh=fine_mesh, in_specs=placed, out_specs=(P(blk), P(blk, None)), check_vma=False
    )
```

time: 587 us -> 226 us (0.39); the launches traced: 581 us -> 226 us
  local copies, waits for them, and re-layouts: 275 us -> 3.68 us
  waiting for transfers between devices: 200 us -> 76.9 us
  Pallas kernels: 0 us -> 62.3 us
  other arithmetic: 24.4 us -> 0.65 us
  blocking collectives: 18.1 us -> 35 us
  matrix products: 14.6 us -> 0 us
    gather x24 -> x0, local copies, waits for them, and re-layouts: 236 us -> none  [the longest x12 141 us: pair_slots(): starts = jnp.searchsorted(sorted_blocks, sorted_blocks, side='left')]
    all_to_all x4, waiting for transfers between devices: 184 us -> 19.9 us  [swap(): return lax.all_to_all(value, axes, split, split, tiled=True)]
    pallas_call x0 -> x14, Pallas kernels: none -> 62.3 us  [run(): pl.pallas_call(kernel, grid=(1,), in_specs=specs, out_specs=out_specs or...]
    all_to_all x0 -> x1, blocking collectives: none -> 35 us  [swap(): return lax.all_to_all(value, axes, split, split, tiled=True)]
    ppermute x0 -> x8, waiting for transfers between devices: none -> 34.3 us  [the longest x4 29.7 us: local(): from_down.append(lax.ppermute(from_down[-1], 'z', up))]
    scatter x4 -> x0, local copies, waits for them, and re-layouts: 33.3 us -> none  [the longest x1 9.13 us: build_send(): filled = jnp.zeros((slot_count,), jnp.bool_).at[pair_index].set(True)]
    all_gather x2 -> x0, blocking collectives: 18.1 us -> none  [the longest x1 9.03 us: local(): lax.all_gather(back_mass, 'hid', axis=1, tiled=True)]
    all_to_all x4, starting transfers between devices: 34.3 us -> 18.7 us  [swap(): return lax.all_to_all(value, axes, split, split, tiled=True)]
  transfers between devices with their start and end apart: 7 -> 16, of which waited for: 3 -> 11; matrix products, arithmetic and copies ran while one was open for 49% -> 0% of each run, Pallas kernels for 0% -> 23%
where the time goes in v1:
time: 226 us
  waiting for transfers between devices  76.9 us (34%)
  Pallas kernels  62.3 us (28%)
  blocking collectives  35 us (15%)
  starting transfers between devices  33.3 us (15%)
  between operations  13.9 us (6%)
  local copies, waits for them, and re-layouts  3.68 us (2%)
    pallas_call x14, Pallas kernels, run(): pl.pallas_call(kernel, grid=(1,), in_specs=specs, out_specs=out_specs or...  62.3 us
    all_to_all x1, blocking collectives, swap(): return lax.all_to_all(value, axes, split, split, tiled=True)  35 us
    ppermute x4, waiting for transfers between devices, local(): from_down.append(lax.ppermute(from_down[-1], 'z', up))  29.7 us
    all_to_all x4, waiting for transfers between devices, swap(): return lax.all_to_all(value, axes, split, split, tiled=True)  19.9 us
    all_to_all x4, starting transfers between devices, swap(): return lax.all_to_all(value, axes, split, split, tiled=True)  18.7 us
    reduce_scatter x2, waiting for transfers between devices, partial(): return lax.psum_scatter(out, 'hid', scatter_dimension=0, tiled=True)  16.3 us
    ppermute x3, starting transfers between devices, local(): from_up.append(lax.ppermute(from_up[-1], 'z', down))  9.47 us
    reduce_scatter x1, waiting for transfers between devices, local(): lax.psum_scatter(fine(rows_near), 'hid', scatter_dimension=0, tiled=True)  5.55 us
  transfers between devices with their start and end apart: 16, of which 11 were waited for; matrix products, arithmetic and copies ran while one was open for 0% of the time, Pallas kernels for 23%

profile of v1, /device:TPU:1, one launch (start us, length us, event | category | flops | bytes accessed | tf_op | source)
XLA Modules:
  0.0 225.6 jit_solution(16453481190561673253)
XLA Ops:
  7.2 0.0 all-gather.2.cloned.1.call-start
  7.2 0.7 all-gather.2.cloned.1.call-update
  7.9 0.0 reduce-scatter.6.cloned.1.call-start
  7.9 2.3 %shard_map.86.a_ref.i0 = bf16[272,1024]{1,0:T(8,128)(2,1)} custom-call(bf16[256,1024]{1,0:T(8,128)(2,1)} %f_ref.1, s32[8,256]{1,0:T(8,128)} %bitcast.18, s32[1,256]{1,0:T(1,128)} %bitcast.21, s32[1,256]{1,0:T(1,128)} %bitcast.22, s32[1,512]{1,0:T(1,128)} %bitcast.20), custom_call_target="tpu_custom_call" | custom-call | tf_op jit(solution)/shard_map/pallas_call | solution.py:347
  10.2 2.5 %collective-permute-start.1 = (bf16[272,1024]{1,0:T(8,128)(2,1)}, bf16[272,1024]{1,0:T(8,128)(2,1)S(1)}, u32[]{:S(2)}, u32[]{:S(2)}) collective-permute-start(bf16[272,1024]{1,0:T(8,128)(2,1)} %shard_map.86.a_ref.i0), channel_id=1, source_target_pairs={{0,2},{2,4},{4,6},{6,8},{8,10},{10,12},{12,14},{14,0},{1,3},{3,5},... | collective-permute-start | bytes 1671176 | tf_op jit(solution)/shard_map/ppermute | solution.py:374
  12.7 3.9 %collective-permute-start.5 = (bf16[272,1024]{1,0:T(8,128)(2,1)}, bf16[272,1024]{1,0:T(8,128)(2,1)S(1)}, u32[]{:S(2)}, u32[]{:S(2)}) collective-permute-start(bf16[272,1024]{1,0:T(8,128)(2,1)} %shard_map.86.a_ref.i0), channel_id=1, source_target_pairs={{0,14},{2,0},{4,2},{6,4},{8,6},{10,8},{12,10},{14,12},{1,15},{3,1}... | collective-permute-start | bytes 1671176 | tf_op jit(solution)/shard_map/ppermute | solution.py:373
  16.7 12.6 %collective-permute-done.1.a_ref.c_ref.i2 = bf16[272,1024]{1,0:T(8,128)(2,1)S(1)} collective-permute-done((bf16[272,1024]{1,0:T(8,128)(2,1)}, bf16[272,1024]{1,0:T(8,128)(2,1)S(1)}, u32[]{:S(2)}, u32[]{:S(2)}) %collective-permute-start.1) | collective-permute-done | bytes 557088 | tf_op jit(solution)/shard_map/ppermute | solution.py:374
  29.2 0.0 copy-start.3
  29.2 0.0 collective-permute-start.2
  29.2 0.0 collective-permute-done.5.b_ref.i1
  29.2 0.0 copy-start.5
  29.2 2.7 %collective-permute-start.6 = (bf16[272,1024]{1,0:T(8,128)(2,1)S(1)}, bf16[272,1024]{1,0:T(8,128)(2,1)S(1)}, u32[]{:S(2)}, u32[]{:S(2)}) collective-permute-start(bf16[272,1024]{1,0:T(8,128)(2,1)S(1)} %collective-permute-done.5.b_ref.i1), channel_id=1, source_target_pairs={{0,14},{2,0},{4,2},{6,4},{8,6},{10,8},{12,10},{14,12},{1,15},{3,1}... | collective-permute-start | bytes 1671176 | tf_op jit(solution)/shard_map/ppermute | solution.py:373
  31.9 0.7 pad_add_fusion.at_ref
  32.6 0.0 copy-done.5
  32.6 4.1 %shard_map.87.begun_ref = bf16[4,13,32,1024]{3,2,1,0:T(8,128)(2,1)} custom-call(s32[4]{0:T(128)} %pad_add_fusion.at_ref, bf16[272,1024]{1,0:T(8,128)(2,1)} %shard_map.86.a_ref.i0, bf16[272,1024]{1,0:T(8,128)(2,1)} %copy-done.5), custom_call_target="tpu_custom_call" | custom-call | tf_op jit(solution)/shard_map/pallas_call | solution.py:347
  36.7 6.7 %collective-permute-done.2.a_ref.i0 = bf16[272,1024]{1,0:T(8,128)(2,1)S(1)} collective-permute-done((bf16[272,1024]{1,0:T(8,128)(2,1)S(1)}, bf16[272,1024]{1,0:T(8,128)(2,1)S(1)}, u32[]{:S(2)}, u32[]{:S(2)}) %collective-permute-start.2) | collective-permute-done | bytes 557088 | tf_op jit(solution)/shard_map/ppermute | solution.py:374
  43.3 0.0 collective-permute-done.6.b_ref.d_ref.i3
  43.3 0.0 copy-done.3
  43.3 0.0 copy-start.6
  43.3 0.8 copy-done.6
  44.2 4.1 %shard_map.88 = bf16[4,13,32,1024]{3,2,1,0:T(8,128)(2,1)} custom-call(s32[4]{0:T(128)} %pad_add_fusion.at_ref, bf16[272,1024]{1,0:T(8,128)(2,1)} %copy-done.3, bf16[272,1024]{1,0:T(8,128)(2,1)} %copy-done.6, bf16[4,13,32,1024]{3,2,1,0:T(8,128)(2,1)} %shard_map.87.begun_ref), custom_call_target="tpu_custom_call", output_to_operand_aliasing={{}: (3, {})} | custom-call | tf_op jit(solution)/shard_map/pallas_call | solution.py:347
  48.3 0.0 copy-done.4
  48.3 4.6 %shard_map.89 = f32[512,1024]{1,0:T(8,128)} custom-call(bf16[272,1024]{1,0:T(8,128)(2,1)} %shard_map.86.a_ref.i0, bf16[272,1024]{1,0:T(8,128)(2,1)} %copy-done.5, bf16[272,1024]{1,0:T(8,128)(2,1)} %copy-done.3, bf16[272,1024]{1,0:T(8,128)(2,1)} %copy-done.6, bf16[512,1024]{1,0:T(8,128)(2,1)} %all-gather.2.cloned.1.call-done.w_ref), custom_call_target="tpu_custom_call" | custom-call | tf_op jit(solution)/shard_map/pallas_call | solution.py:347
  52.9 0.0 reduce-scatter.6.cloned.1.call-update
  52.9 4.0 %all-to-all-start.1 = ((bf16[4,13,32,1024]{3,2,1,0:T(8,128)(2,1)}), bf16[4,13,32,1024]{3,2,1,0:T(8,128)(2,1)S(1)}, u32[]{:S(2)}, u32[]{:S(2)}) async-start(bf16[4,13,32,1024]{3,2,1,0:T(8,128)(2,1)} %shard_map.88), calls=%async_computation.1 | async-start | bytes 6815744 | tf_op jit(solution)/shard_map/all_to_all | solution.py:333
  56.9 0.0 reduce-scatter.4.cloned.1.call-start
  56.9 0.0 collective-permute-start.3
  57.0 2.5 %collective-permute-start = (bf16[8,1024,256]{2,1,0:T(8,128)(2,1)}, bf16[8,1024,256]{2,1,0:T(8,128)(2,1)}, u32[]{:S(2)}, u32[]{:S(2)}) collective-permute-start(bf16[8,1024,256]{2,1,0:T(8,128)(2,1)} %own_ref.3), channel_id=1, source_target_pairs={{0,1},{1,0},{2,3},{3,2},{4,5},{5,4},{6,7},{7,6},{8,9},{9,8},{10,11... | collective-permute-start | bytes 12582920 | tf_op jit(solution)/shard_map/ppermute | solution.py:375
  59.5 2.9 %collective-permute-start.7 = (bf16[272,1024]{1,0:T(8,128)(2,1)}, bf16[272,1024]{1,0:T(8,128)(2,1)S(1)}, u32[]{:S(2)}, u32[]{:S(2)}) collective-permute-start(bf16[272,1024]{1,0:T(8,128)(2,1)} %copy-done.6), channel_id=1, source_target_pairs={{0,14},{2,0},{4,2},{6,4},{8,6},{10,8},{12,10},{14,12},{1,15},{3,1}... | collective-permute-start | bytes 1671176 | tf_op jit(solution)/shard_map/ppermute | solution.py:373
  62.3 7.8 %collective-permute-done.3.a_ref.c_ref.i2 = bf16[272,1024]{1,0:T(8,128)(2,1)S(1)} collective-permute-done((bf16[272,1024]{1,0:T(8,128)(2,1)}, bf16[272,1024]{1,0:T(8,128)(2,1)S(1)}, u32[]{:S(2)}, u32[]{:S(2)}) %collective-permute-start.3) | collective-permute-done | bytes 557088 | tf_op jit(solution)/shard_map/ppermute | solution.py:374
  70.2 0.0 collective-permute-start.4
  70.2 4.6 %collective-permute-done.7.b_ref.i1 = bf16[272,1024]{1,0:T(8,128)(2,1)S(1)} collective-permute-done((bf16[272,1024]{1,0:T(8,128)(2,1)}, bf16[272,1024]{1,0:T(8,128)(2,1)S(1)}, u32[]{:S(2)}, u32[]{:S(2)}) %collective-permute-start.7) | collective-permute-done | bytes 557088 | tf_op jit(solution)/shard_map/ppermute | solution.py:373
  74.8 0.8 copy-done.8
  75.6 4.1 %shard_map.90.begun_ref = bf16[4,13,32,1024]{3,2,1,0:T(8,128)(2,1)} custom-call(s32[4]{0:T(128)} %pad_add_fusion.at_ref, bf16[272,1024]{1,0:T(8,128)(2,1)} %copy-done.4, bf16[272,1024]{1,0:T(8,128)(2,1)} %copy-done.8), custom_call_target="tpu_custom_call" | custom-call | tf_op jit(solution)/shard_map/pallas_call | solution.py:347
  79.7 2.7 %collective-permute-done.4.b_ref.d_ref.i3 = bf16[272,1024]{1,0:T(8,128)(2,1)S(1)} collective-permute-done((bf16[272,1024]{1,0:T(8,128)(2,1)S(1)}, bf16[272,1024]{1,0:T(8,128)(2,1)S(1)}, u32[]{:S(2)}, u32[]{:S(2)}) %collective-permute-start.4) | collective-permute-done | bytes 557088 | tf_op jit(solution)/shard_map/ppermute | solution.py:374
  82.3 0.0 copy-done.7
  82.3 0.8 copy-done.9
  83.2 4.1 %shard_map.91 = bf16[4,13,32,1024]{3,2,1,0:T(8,128)(2,1)} custom-call(s32[4]{0:T(128)} %pad_add_fusion.at_ref, bf16[272,1024]{1,0:T(8,128)(2,1)} %copy-done.7, bf16[272,1024]{1,0:T(8,128)(2,1)} %copy-done.9, bf16[4,13,32,1024]{3,2,1,0:T(8,128)(2,1)} %shard_map.90.begun_ref), custom_call_target="tpu_custom_call", output_to_operand_aliasing={{}: (3, {})} | custom-call | tf_op jit(solution)/shard_map/pallas_call | solution.py:347
  87.3 7.6 %all-to-all-done.1.r_ref.meta_ref = bf16[4,13,32,1024]{3,2,1,0:T(8,128)(2,1)S(1)} async-done(((bf16[4,13,32,1024]{3,2,1,0:T(8,128)(2,1)}), bf16[4,13,32,1024]{3,2,1,0:T(8,128)(2,1)S(1)}, u32[]{:S(2)}, u32[]{:S(2)}) %all-to-all-start.1) | async-done | bytes 3407904 | tf_op jit(solution)/shard_map/all_to_all | solution.py:333
  94.9 5.7 %shard_map.92 = f32[512,1024]{1,0:T(8,128)} custom-call(bf16[272,1024]{1,0:T(8,128)(2,1)} %copy-done.4, bf16[272,1024]{1,0:T(8,128)(2,1)} %copy-done.8, bf16[272,1024]{1,0:T(8,128)(2,1)} %copy-done.7, bf16[272,1024]{1,0:T(8,128)(2,1)} %copy-done.9, bf16[512,1024]{1,0:T(8,128)(2,1)} %all-gather.2.cloned.1.call-done.w_ref), custom_call_target="tpu_custom_call" | custom-call | tf_op jit(solution)/shard_map/pallas_call | solution.py:347
  100.6 0.0 reduce-scatter.4.cloned.1.call-update
  100.7 0.0 copy-done
  100.7 3.7 %all-to-all-start = ((bf16[4,13,32,1024]{3,2,1,0:T(8,128)(2,1)}), bf16[4,13,32,1024]{3,2,1,0:T(8,128)(2,1)S(1)}, u32[]{:S(2)}, u32[]{:S(2)}) async-start(bf16[4,13,32,1024]{3,2,1,0:T(8,128)(2,1)} %shard_map.91), calls=%async_computation | async-start | bytes 6815744 | tf_op jit(solution)/shard_map/all_to_all | solution.py:333
  104.4 0.0 reduce-scatter.8.cloned.1.call-start
  104.5 0.0 collective-permute-done.peer_ref
  104.5 10.1 %shard_map.93 = f32[4,2,6,32,256]{4,3,2,1,0:T(8,128)} custom-call(bf16[8,1024,256]{2,1,0:T(8,128)(2,1)} %own_ref.3, bf16[8,1024,256]{2,1,0:T(8,128)(2,1)} %collective-permute-done.peer_ref, bf16[4,13,32,1024]{3,2,1,0:T(8,128)(2,1)} %copy-done), custom_call_target="tpu_custom_call" | custom-call | flops 8000000000 | bytes 41943040 | tf_op jit(solution)/shard_map/pallas_call | solution.py:347
  114.6 0.0 reduce-scatter.8.cloned.1.call-update
  114.6 0.0 reduce-scatter.6.cloned.1.call-done.c_ref
  114.6 2.4 %shard_map.94.first_ref = f32[4,16,256]{2,1,0:T(8,128)} custom-call(s32[4]{0:T(128)} %pad_add_fusion.at_ref, f32[128,1024]{1,0:T(8,128)} %reduce-scatter.6.cloned.1.call-done.c_ref, bf16[272,1024]{1,0:T(8,128)(2,1)} %shard_map.86.a_ref.i0, bf16[272,1024]{1,0:T(8,128)(2,1)} %copy-done.5, bf16[272,1024]{1,0:T(8,128)(2,1)} %copy-done.3, bf16[272,1024]{1,0:T(8,128)(2,1)} %copy-done.6), custom_call_target="tpu_custom_call" | custom-call | tf_op jit(solution)/shard_map/pallas_call | solution.py:347
  117.1 16.3 %reduce-scatter.4.cloned.1.call-done.c_ref = f32[128,1024]{1,0:T(8,128)} async-done(((f32[512,1024]{1,0:T(8,128)}), f32[128,1024]{1,0:T(8,128)}) %reduce-scatter.4.cloned.1.call-update) | async-done | bytes 524304 | tf_op jit(solution)/shard_map/reduce_scatter | solution.py:424
  133.4 2.6 %shard_map.95 = f32[4,8,16,256]{3,2,1,0:T(8,128)} custom-call(s32[4]{0:T(128)} %pad_add_fusion.at_ref, f32[128,1024]{1,0:T(8,128)} %reduce-scatter.4.cloned.1.call-done.c_ref, bf16[272,1024]{1,0:T(8,128)(2,1)} %copy-done.4, bf16[272,1024]{1,0:T(8,128)(2,1)} %copy-done.8, bf16[272,1024]{1,0:T(8,128)(2,1)} %copy-done.7, bf16[272,1024]{1,0:T(8,128)(2,1)} %copy-done.9, ...), custom_call_target="tpu_custom_call" | custom-call | tf_op jit(solution)/shard_map/pallas_call | solution.py:347
  136.0 5.4 %all-to-all-done.r_ref.meta_ref = bf16[4,13,32,1024]{3,2,1,0:T(8,128)(2,1)S(1)} async-done(((bf16[4,13,32,1024]{3,2,1,0:T(8,128)(2,1)}), bf16[4,13,32,1024]{3,2,1,0:T(8,128)(2,1)S(1)}, u32[]{:S(2)}, u32[]{:S(2)}) %all-to-all-start) | async-done | bytes 3407904 | tf_op jit(solution)/shard_map/all_to_all | solution.py:333
  141.4 7.4 %all-to-all-start.2 = ((f32[32,16,256]{2,1,0:T(8,128)}), f32[32,16,256]{2,1,0:T(8,128)}, u32[]{:S(2)}, u32[]{:S(2)}) async-start(f32[32,16,256]{2,1,0:T(8,128)} %bitcast.14), calls=%async_computation.4 | async-start | bytes 1048576 | tf_op jit(solution)/shard_map/all_to_all | solution.py:333
  148.8 0.0 copy-done.1
  148.8 10.2 %shard_map.96 = f32[4,2,6,32,256]{4,3,2,1,0:T(8,128)} custom-call(bf16[8,1024,256]{2,1,0:T(8,128)(2,1)} %own_ref.3, bf16[8,1024,256]{2,1,0:T(8,128)(2,1)} %collective-permute-done.peer_ref, bf16[4,13,32,1024]{3,2,1,0:T(8,128)(2,1)} %copy-done.1), custom_call_target="tpu_custom_call" | custom-call | flops 8000000000 | bytes 41943040 | tf_op jit(solution)/shard_map/pallas_call | solution.py:347
  159.0 1.1 all-to-all-done.2.coarse_ref
  160.1 3.6 %all-to-all-start.3 = ((f32[4,2,6,32,256]{4,3,2,1,0:T(8,128)}), f32[4,2,6,32,256]{4,3,2,1,0:T(8,128)S(1)}, u32[]{:S(2)}, u32[]{:S(2)}) async-start(f32[4,2,6,32,256]{4,3,2,1,0:T(8,128)} %shard_map.96), calls=%async_computation.5 | async-start | bytes 3145728 | tf_op jit(solution)/shard_map/all_to_all | solution.py:333
  163.7 5.5 %reduce-scatter.8.cloned.1.call-done.y_ref = f32[1,2,6,32,256]{4,3,2,1,0:T(8,128)} async-done(((f32[4,2,6,32,256]{4,3,2,1,0:T(8,128)}), f32[1,2,6,32,256]{4,3,2,1,0:T(8,128)}) %reduce-scatter.8.cloned.1.call-update) | async-done | bytes 393232 | tf_op jit(solution)/shard_map/reduce_scatter | solution.py:469
  169.2 2.1 shard_map.97.first_ref
  171.4 5.8 %all-to-all-done.3.y_ref = f32[4,2,6,32,256]{4,3,2,1,0:T(8,128)S(1)} async-done(((f32[4,2,6,32,256]{4,3,2,1,0:T(8,128)}), f32[4,2,6,32,256]{4,3,2,1,0:T(8,128)S(1)}, u32[]{:S(2)}, u32[]{:S(2)}) %all-to-all-start.3) | async-done | bytes 1572896 | tf_op jit(solution)/shard_map/all_to_all | solution.py:333
  177.2 1.2 copy-done.2
  178.4 2.6 %shard_map.98 = f32[512,128]{1,0:T(8,128)} custom-call(s32[4]{0:T(128)} %pad_add_fusion.at_ref, f32[4,2,6,32,256]{4,3,2,1,0:T(8,128)} %copy-done.2, bf16[4,13,32,1024]{3,2,1,0:T(8,128)(2,1)} %copy-done.1, f32[8,256]{1,0:T(8,128)} %shard_map.97.first_ref), custom_call_target="tpu_custom_call" | custom-call | tf_op jit(solution)/shard_map/pallas_call | solution.py:347
  181.0 35.0 %all_to_all.31 = f32[256,2,128]{2,1,0:T(2,128)} all-to-all(f32[256,2,128]{2,1,0:T(2,128)} %bitcast.16), channel_id=1, replica_groups=mesh['hid'=4,'x'=4,'z'=8,'c'=2] {'hid','x','z','c'}, dimensions={0} | all-to-all | bytes 524288 | tf_op jit(solution)/shard_map/all_to_all | solution.py:333
  216.0 3.1 %shard_map.99 = (f32[1,256]{1,0:T(1,128)}, f32[8,256]{1,0:T(8,128)}) custom-call(s32[4]{0:T(128)} %pad_add_fusion.at_ref, f32[512,128]{1,0:T(8,128)} %bitcast.15, f32[32,16,256]{2,1,0:T(8,128)} %all-to-all-done.2.coarse_ref, s32[8,256]{1,0:T(8,128)} %bitcast.19), custom_call_target="tpu_custom_call" | custom-call | tf_op jit(solution)/shard_map/pallas_call | solution.py:347
  (8 shorter events, 0.0 us)
Async XLA Ops:
  7.2 41.1 %all-gather.2.cloned.1.call-start = ((), (), s32[]{:S(2)}) async-start(), calls=%async_computation.8 | async-start | bytes 1179648 | tf_op jit(solution)/shard_map/all_gather | solution.py:376
  7.9 106.7 %reduce-scatter.6.cloned.1.call-start = ((), (), s32[]{:S(2)}) async-start(), calls=%async_computation.10 | async-start | bytes 2621440 | tf_op jit(solution)/shard_map/reduce_scatter | solution.py:424
  10.2 19.0 %collective-permute-start.1 = (bf16[272,1024]{1,0:T(8,128)(2,1)}, bf16[272,1024]{1,0:T(8,128)(2,1)S(1)}, u32[]{:S(2)}, u32[]{:S(2)}) collective-permute-start(bf16[272,1024]{1,0:T(8,128)(2,1)} %shard_map.86.a_ref.i0), channel_id=1, source_target_pairs={{0,2},{2,4},{4,6},{6,8},{8,10},{10,12},{12,14},{14,0},{1,3},{3,5},... | collective-permute-start | bytes 1671176 | tf_op jit(solution)/shard_map/ppermute | solution.py:374
  12.7 16.5 %collective-permute-start.5 = (bf16[272,1024]{1,0:T(8,128)(2,1)}, bf16[272,1024]{1,0:T(8,128)(2,1)S(1)}, u32[]{:S(2)}, u32[]{:S(2)}) collective-permute-start(bf16[272,1024]{1,0:T(8,128)(2,1)} %shard_map.86.a_ref.i0), channel_id=1, source_target_pairs={{0,14},{2,0},{4,2},{6,4},{8,6},{10,8},{12,10},{14,12},{1,15},{3,1}... | collective-permute-start | bytes 1671176 | tf_op jit(solution)/shard_map/ppermute | solution.py:373
  29.2 14.1 %copy-start.3 = (bf16[272,1024]{1,0:T(8,128)(2,1)}, bf16[272,1024]{1,0:T(8,128)(2,1)S(1)}, u32[]{:S(2)}) copy-start(bf16[272,1024]{1,0:T(8,128)(2,1)S(1)} %collective-permute-done.1.a_ref.c_ref.i2) | copy-start | bytes 1671172
  29.2 14.1 %collective-permute-start.2 = (bf16[272,1024]{1,0:T(8,128)(2,1)S(1)}, bf16[272,1024]{1,0:T(8,128)(2,1)S(1)}, u32[]{:S(2)}, u32[]{:S(2)}) collective-permute-start(bf16[272,1024]{1,0:T(8,128)(2,1)S(1)} %collective-permute-done.1.a_ref.c_ref.i2), channel_id=1, source_target_pairs={{0,2},{2,4},{4,6},{6,8},{8,10},{10,12},{12,14},{14,0},{1,3},{3,5},... | collective-permute-start | bytes 1671176 | tf_op jit(solution)/shard_map/ppermute | solution.py:374
  29.2 3.3 %copy-start.5 = (bf16[272,1024]{1,0:T(8,128)(2,1)}, bf16[272,1024]{1,0:T(8,128)(2,1)S(1)}, u32[]{:S(2)}) copy-start(bf16[272,1024]{1,0:T(8,128)(2,1)S(1)} %collective-permute-done.5.b_ref.i1) | copy-start | bytes 1671172
  29.2 14.1 %collective-permute-start.6 = (bf16[272,1024]{1,0:T(8,128)(2,1)S(1)}, bf16[272,1024]{1,0:T(8,128)(2,1)S(1)}, u32[]{:S(2)}, u32[]{:S(2)}) collective-permute-start(bf16[272,1024]{1,0:T(8,128)(2,1)S(1)} %collective-permute-done.5.b_ref.i1), channel_id=1, source_target_pairs={{0,14},{2,0},{4,2},{6,4},{8,6},{10,8},{12,10},{14,12},{1,15},{3,1}... | collective-permute-start | bytes 1671176 | tf_op jit(solution)/shard_map/ppermute | solution.py:373
  43.3 5.0 %copy-start.4 = (bf16[272,1024]{1,0:T(8,128)(2,1)}, bf16[272,1024]{1,0:T(8,128)(2,1)S(1)}, u32[]{:S(2)}) copy-start(bf16[272,1024]{1,0:T(8,128)(2,1)S(1)} %collective-permute-done.2.a_ref.i0) | copy-start | bytes 1671172
  43.3 0.8 copy-start.6
  52.9 42.0 %all-to-all-start.1 = ((bf16[4,13,32,1024]{3,2,1,0:T(8,128)(2,1)}), bf16[4,13,32,1024]{3,2,1,0:T(8,128)(2,1)S(1)}, u32[]{:S(2)}, u32[]{:S(2)}) async-start(bf16[4,13,32,1024]{3,2,1,0:T(8,128)(2,1)} %shard_map.88), calls=%async_computation.1 | async-start | bytes 6815744 | tf_op jit(solution)/shard_map/all_to_all | solution.py:333
  56.9 76.4 %reduce-scatter.4.cloned.1.call-start = ((), (), s32[]{:S(2)}) async-start(), calls=%async_computation.9 | async-start | bytes 2621440 | tf_op jit(solution)/shard_map/reduce_scatter | solution.py:424
  56.9 13.2 %collective-permute-start.3 = (bf16[272,1024]{1,0:T(8,128)(2,1)}, bf16[272,1024]{1,0:T(8,128)(2,1)S(1)}, u32[]{:S(2)}, u32[]{:S(2)}) collective-permute-start(bf16[272,1024]{1,0:T(8,128)(2,1)} %copy-done.4), channel_id=1, source_target_pairs={{0,2},{2,4},{4,6},{6,8},{8,10},{10,12},{12,14},{14,0},{1,3},{3,5},... | collective-permute-start | bytes 1671176 | tf_op jit(solution)/shard_map/ppermute | solution.py:374
  57.0 47.5 %collective-permute-start = (bf16[8,1024,256]{2,1,0:T(8,128)(2,1)}, bf16[8,1024,256]{2,1,0:T(8,128)(2,1)}, u32[]{:S(2)}, u32[]{:S(2)}) collective-permute-start(bf16[8,1024,256]{2,1,0:T(8,128)(2,1)} %own_ref.3), channel_id=1, source_target_pairs={{0,1},{1,0},{2,3},{3,2},{4,5},{5,4},{6,7},{7,6},{8,9},{9,8},{10,11... | collective-permute-start | bytes 12582920 | tf_op jit(solution)/shard_map/ppermute | solution.py:375
  59.5 15.3 %collective-permute-start.7 = (bf16[272,1024]{1,0:T(8,128)(2,1)}, bf16[272,1024]{1,0:T(8,128)(2,1)S(1)}, u32[]{:S(2)}, u32[]{:S(2)}) collective-permute-start(bf16[272,1024]{1,0:T(8,128)(2,1)} %copy-done.6), channel_id=1, source_target_pairs={{0,14},{2,0},{4,2},{6,4},{8,6},{10,8},{12,10},{14,12},{1,15},{3,1}... | collective-permute-start | bytes 1671176 | tf_op jit(solution)/shard_map/ppermute | solution.py:373
  70.2 12.2 %copy-start.7 = (bf16[272,1024]{1,0:T(8,128)(2,1)}, bf16[272,1024]{1,0:T(8,128)(2,1)S(1)}, u32[]{:S(2)}) copy-start(bf16[272,1024]{1,0:T(8,128)(2,1)S(1)} %collective-permute-done.3.a_ref.c_ref.i2) | copy-start | bytes 1671172
  70.2 12.2 %collective-permute-start.4 = (bf16[272,1024]{1,0:T(8,128)(2,1)S(1)}, bf16[272,1024]{1,0:T(8,128)(2,1)S(1)}, u32[]{:S(2)}, u32[]{:S(2)}) collective-permute-start(bf16[272,1024]{1,0:T(8,128)(2,1)S(1)} %collective-permute-done.3.a_ref.c_ref.i2), channel_id=1, source_target_pairs={{0,2},{2,4},{4,6},{6,8},{8,10},{10,12},{12,14},{14,0},{1,3},{3,5},... | collective-permute-start | bytes 1671176 | tf_op jit(solution)/shard_map/ppermute | solution.py:374
  74.8 0.8 copy-start.8
  82.3 0.8 copy-start.9
  94.9 5.7 %copy-start = (bf16[4,13,32,1024]{3,2,1,0:T(8,128)(2,1)}, bf16[4,13,32,1024]{3,2,1,0:T(8,128)(2,1)S(1)}, u32[]{:S(2)}) copy-start(bf16[4,13,32,1024]{3,2,1,0:T(8,128)(2,1)S(1)} %all-to-all-done.1.r_ref.meta_ref) | copy-start | bytes 10223620
  100.7 40.8 %all-to-all-start = ((bf16[4,13,32,1024]{3,2,1,0:T(8,128)(2,1)}), bf16[4,13,32,1024]{3,2,1,0:T(8,128)(2,1)S(1)}, u32[]{:S(2)}, u32[]{:S(2)}) async-start(bf16[4,13,32,1024]{3,2,1,0:T(8,128)(2,1)} %shard_map.91), calls=%async_computation | async-start | bytes 6815744 | tf_op jit(solution)/shard_map/all_to_all | solution.py:333
  104.4 64.8 %reduce-scatter.8.cloned.1.call-start = ((), (), s32[]{:S(2)}) async-start(), calls=%async_computation.11 | async-start | bytes 1966080 | tf_op jit(solution)/shard_map/reduce_scatter | solution.py:469
  141.4 7.4 %copy-start.1 = (bf16[4,13,32,1024]{3,2,1,0:T(8,128)(2,1)}, bf16[4,13,32,1024]{3,2,1,0:T(8,128)(2,1)S(1)}, u32[]{:S(2)}) copy-start(bf16[4,13,32,1024]{3,2,1,0:T(8,128)(2,1)S(1)} %all-to-all-done.r_ref.meta_ref) | copy-start | bytes 10223620
  141.4 18.7 %all-to-all-start.2 = ((f32[32,16,256]{2,1,0:T(8,128)}), f32[32,16,256]{2,1,0:T(8,128)}, u32[]{:S(2)}, u32[]{:S(2)}) async-start(f32[32,16,256]{2,1,0:T(8,128)} %bitcast.14), calls=%async_computation.4 | async-start | bytes 1048576 | tf_op jit(solution)/shard_map/all_to_all | solution.py:333
  160.1 17.1 %all-to-all-start.3 = ((f32[4,2,6,32,256]{4,3,2,1,0:T(8,128)}), f32[4,2,6,32,256]{4,3,2,1,0:T(8,128)S(1)}, u32[]{:S(2)}, u32[]{:S(2)}) async-start(f32[4,2,6,32,256]{4,3,2,1,0:T(8,128)} %shard_map.96), calls=%async_computation.5 | async-start | bytes 3145728 | tf_op jit(solution)/shard_map/all_to_all | solution.py:333
  177.2 1.2 copy-start.2
Sparse Core Ops, SparseCore 0:
  9.9 30.0 all-gather.1
  53.0 33.7 reduce-scatter.5
  100.8 32.5 reduce-scatter.3
  135.8 33.3 reduce-scatter.7

commit v2 on v1

--- a/solution.py
+++ b/solution.py
@@ -243,17 +243,33 @@
         out_ref[s] = lines
 
 
-def coarse_last_kernel(at_ref, c_ref, i0, i1, i2, i3, first_ref, out_ref):
-    z = at_ref[1]
+def coarse_last_kernel(at_ref, c_ref, i0, i1, i2, i3, first_ref, *out_refs):
     last = coarse_lines(at_ref, c_ref, (i0, i1, i2, i3))
-    away = [d for four in AWAY for d in four]
-    for i in range(NZ):
-        lines = first_ref[i] if i < NZ // 2 else last[i - NZ // 2]
-        for d in range(HID):
-            out_ref[d, (z + NZ + away[i]) & (NZ - 1)] = lines
-
-
-def finish_kernel(at_ref, fine_ref, coarse_ref, routes_ref, loss_ref, prob_ref):
+    for i, out_ref in enumerate(out_refs):
+        out_ref[...] = first_ref[i] if i < NZ // 2 else last[i - NZ // 2]
+
+
+def joined(shards):
+    top = shards[0][0:1]
+    for shard in shards[1:]:
+        top = jnp.maximum(top, shard[0:1])
+    sums = [shard[1:2] * jnp.exp(shard[0:1] - top) for shard in shards]
+    picks = [shard[8:16] for shard in shards]
+    while len(sums) > 1:
+        sums = [a + b for a, b in zip(sums[0::2], sums[1::2])]
+        picks = [a + b for a, b in zip(picks[0::2], picks[1::2])]
+    return top, sums[0], picks[0]
+
+
+def coarse_sum_kernel(*refs):
+    *shard_refs, out_ref = refs
+    top, total, picked = joined([ref[...] for ref in shard_refs])
+    out_ref[0:8, :] = jnp.concatenate([top, total, jnp.zeros((6, ROWS), F32)], axis=0)
+    out_ref[8:16, :] = picked
+
+
+def finish_kernel(at_ref, fine_ref, *refs):
+    *coarse_refs, routes_ref, loss_ref, prob_ref = refs
     x, core = at_ref[0], at_ref[2]
     routes = routes_ref[...]
     chips = NX * NZ
@@ -306,12 +322,8 @@
     log_prob = pair - fine_lse
     prob = jnp.exp(log_prob)
 
-    parts = coarse_ref[...]
-    tops = parts[:, 0, :]
-    peak = jnp.max(tops, axis=0, keepdims=True)
-    total = jnp.sum(parts[:, 1, :] * jnp.exp(tops - peak), axis=0, keepdims=True)
-    coarse_lse = peak + jnp.log(total)
-    picked = jnp.sum(parts[:, 8:16, :], axis=0) - coarse_lse
+    top, total, picked = joined([ref[...] for ref in coarse_refs])
+    picked = picked - (top + jnp.log(total))
     kl = jnp.sum(prob * (log_prob - picked), axis=0, keepdims=True)
     loss_ref[...] = fine_lse - target + kl
     prob_ref[...] = prob
@@ -383,8 +395,9 @@
 
     def in_turn(call, first, *more):
         first, _ = lax.optimization_barrier((first, last_run[0]))
-        (last_run[0],) = call(first, *more)
-        return last_run[0]
+        outs = call(first, *more)
+        last_run[0] = outs[0]
+        return outs if len(outs) > 1 else outs[0]
 
     def select(four, *waits):
         out = shape((NX, tiers, FOUR, PART), BF16)
@@ -468,11 +481,27 @@
     part_far = partial(far, rows_near)
     fine_near = lax.psum_scatter(fine(rows_near), "hid", scatter_dimension=0, tiled=True)
     lines = coarse(coarse_kernel, part_near, near, shape((NZ // 2, 16, ROWS), F32))
-    lines = coarse(coarse_last_kernel, part_far, far, shape((HID, NZ, 16, ROWS), F32), lines)
-    lines = swap(lines.reshape(HID * NZ, 16, ROWS), ("hid", "z"))
-    fine_far, lines = lax.optimization_barrier((fine(rows_far), lines))
+    lines = coarse(
+        coarse_last_kernel, part_far, far, [shape((16, ROWS), F32)] * NZ, lines
+    )
+    away = [d for four in AWAY for d in four]
+    lines = [
+        lax.ppermute(part, "z", [(i, (i + d) % NZ) for i in range(NZ)]) if d else part
+        for part, d in zip(lines, away)
+    ]
+    early = 4
+    rows_far, *lines[:early] = lax.optimization_barrier((rows_far, *lines[:early]))
+    fine_far = fine(rows_far)
+    lines[0], _ = lax.optimization_barrier((lines[0], fine_far))
+    (own,) = run(coarse_sum_kernel, [None] * NZ, shape((16, ROWS), F32), *lines)
+    last_run[0] = own
+    across, following, before = (
+        lax.ppermute(own, "hid", [(i, (i + d) % HID) for i in range(HID)]) for d in (2, 1, 3)
+    )
+    lines = [own, across, following, before]
     fine_far = swap(fine_far, "hid")
     first = scored(score_kernel, fine_near, rows_near, shape((8, LBL), F32))
+    fine_far, *lines = lax.optimization_barrier((fine_far, *lines))
     table = scored(
         score_last_kernel, fine_far, rows_far, shape((HID * NX * NZ * NC * NC, 128), F32), first
     )
@@ -480,11 +509,11 @@
 
     loss, prob = run(
         finish_kernel,
-        [smem(), None, None, None],
+        [smem()] + [None] * (HID + 2),
         [shape((1, ROWS), F32), shape((TOP, ROWS), F32)],
         at,
         table,
-        lines,
+        *lines,
         routes_t,
     )
     return loss.reshape(ROWS), prob.T

time: 226 us -> 227 us (level)
  starting transfers between devices: 33.3 us -> 43.6 us
  waiting for transfers between devices: 76.9 us -> 67.5 us
  blocking collectives: 35 us -> 32.5 us
    ppermute x0 -> x10, starting transfers between devices: none -> 17.7 us  [the longest x7 13.4 us: local(): lax.ppermute(part, 'z', [(i, (i + d) % NZ) for i in range(NZ)])]
    all_to_all x4 -> x3, waiting for transfers between devices: 19.9 us -> 9.66 us  [swap(): return lax.all_to_all(value, axes, split, split, tiled=True)]
    all_to_all x4 -> x3, starting transfers between devices: 18.7 us -> 11.3 us  [swap(): return lax.all_to_all(value, axes, split, split, tiled=True)]
    ppermute x0 -> x10, waiting for transfers between devices: none -> 6.32 us  [the longest x7 5.2 us: local(): lax.ppermute(part, 'z', [(i, (i + d) % NZ) for i in range(NZ)])]
    reduce_scatter x1, waiting for transfers between devices: 5.55 us -> 0.01 us  [local(): lax.psum_scatter(fine(rows_near), 'hid', scatter_dimension=0, tiled=True)]
    all_to_all x1, blocking collectives: 35 us -> 32.5 us  [swap(): return lax.all_to_all(value, axes, split, split, tiled=True)]
    pallas_call x14 -> x15, Pallas kernels: 62.3 us -> 63.4 us  [run(): pl.pallas_call(kernel, grid=(1,), in_specs=specs, out_specs=out_specs or...]
  transfers between devices with their start and end apart: 16 -> 25, of which waited for: 11 -> 11; matrix products, arithmetic and copies ran while one was open for 0% -> 0% of each run, Pallas kernels for 23% -> 24%
where the time goes in v2:
time: 227 us; the launch traced here: 226 us
  waiting for transfers between devices  67.5 us (30%)
  Pallas kernels  63.4 us (28%)
  starting transfers between devices  43.6 us (19%)
  blocking collectives  32.5 us (14%)
  between operations  14 us (6%)
  local copies, waits for them, and re-layouts  4.28 us (2%)
    pallas_call x15, Pallas kernels, run(): pl.pallas_call(kernel, grid=(1,), in_specs=specs, out_specs=out_specs or...  63.4 us
    all_to_all x1, blocking collectives, swap(): return lax.all_to_all(value, axes, split, split, tiled=True)  32.5 us
    ppermute x4, waiting for transfers between devices, local(): from_down.append(lax.ppermute(from_down[-1], 'z', up))  29.8 us
    reduce_scatter x2, waiting for transfers between devices, partial(): return lax.psum_scatter(out, 'hid', scatter_dimension=0, tiled=True)  16.4 us
    ppermute x7, starting transfers between devices, local(): lax.ppermute(part, 'z', [(i, (i + d) % NZ) for i in range(NZ)])  13.4 us
    all_to_all x3, starting transfers between devices, swap(): return lax.all_to_all(value, axes, split, split, tiled=True)  11.3 us
    all_to_all x3, waiting for transfers between devices, swap(): return lax.all_to_all(value, axes, split, split, tiled=True)  9.66 us
    ppermute x3, starting transfers between devices, local(): from_up.append(lax.ppermute(from_up[-1], 'z', down))  9.47 us
  transfers between devices with their start and end apart: 25, of which 11 were waited for; matrix products, arithmetic and copies ran while one was open for 0% of the time, Pallas kernels for 24%

profile of v2, /device:TPU:1, one launch (start us, length us, event | category | flops | bytes accessed | tf_op | source)
XLA Modules:
  0.0 225.9 jit_solution(2825266358763997478)
XLA Ops:
  7.2 0.0 all-gather.2.cloned.1.call-start
  7.2 0.7 all-gather.2.cloned.1.call-update
  7.9 0.0 reduce-scatter.6.cloned.1.call-start
  7.9 2.3 %shard_map.86.a_ref.i0 = bf16[272,1024]{1,0:T(8,128)(2,1)} custom-call(bf16[256,1024]{1,0:T(8,128)(2,1)} %f_ref.1, s32[8,256]{1,0:T(8,128)} %bitcast.16, s32[1,256]{1,0:T(1,128)} %bitcast.19, s32[1,256]{1,0:T(1,128)} %bitcast.20, s32[1,512]{1,0:T(1,128)} %bitcast.18), custom_call_target="tpu_custom_call" | custom-call | tf_op jit(solution)/shard_map/pallas_call | solution.py:359
  10.2 2.5 %collective-permute-start.1 = (bf16[272,1024]{1,0:T(8,128)(2,1)}, bf16[272,1024]{1,0:T(8,128)(2,1)S(1)}, u32[]{:S(2)}, u32[]{:S(2)}) collective-permute-start(bf16[272,1024]{1,0:T(8,128)(2,1)} %shard_map.86.a_ref.i0), channel_id=1, source_target_pairs={{0,2},{2,4},{4,6},{6,8},{8,10},{10,12},{12,14},{14,0},{1,3},{3,5},... | collective-permute-start | bytes 1671176 | tf_op jit(solution)/shard_map/ppermute | solution.py:386
  12.7 3.9 %collective-permute-start.5 = (bf16[272,1024]{1,0:T(8,128)(2,1)}, bf16[272,1024]{1,0:T(8,128)(2,1)S(1)}, u32[]{:S(2)}, u32[]{:S(2)}) collective-permute-start(bf16[272,1024]{1,0:T(8,128)(2,1)} %shard_map.86.a_ref.i0), channel_id=1, source_target_pairs={{0,14},{2,0},{4,2},{6,4},{8,6},{10,8},{12,10},{14,12},{1,15},{3,1}... | collective-permute-start | bytes 1671176 | tf_op jit(solution)/shard_map/ppermute | solution.py:385
  16.6 12.6 %collective-permute-done.1.a_ref.c_ref.i2 = bf16[272,1024]{1,0:T(8,128)(2,1)S(1)} collective-permute-done((bf16[272,1024]{1,0:T(8,128)(2,1)}, bf16[272,1024]{1,0:T(8,128)(2,1)S(1)}, u32[]{:S(2)}, u32[]{:S(2)}) %collective-permute-start.1) | collective-permute-done | bytes 557088 | tf_op jit(solution)/shard_map/ppermute | solution.py:386
  29.2 0.0 collective-permute-start.2
  29.2 0.0 collective-permute-done.5.b_ref.i1
  29.2 2.7 %collective-permute-start.6 = (bf16[272,1024]{1,0:T(8,128)(2,1)S(1)}, bf16[272,1024]{1,0:T(8,128)(2,1)S(1)}, u32[]{:S(2)}, u32[]{:S(2)}) collective-permute-start(bf16[272,1024]{1,0:T(8,128)(2,1)S(1)} %collective-permute-done.5.b_ref.i1), channel_id=1, source_target_pairs={{0,14},{2,0},{4,2},{6,4},{8,6},{10,8},{12,10},{14,12},{1,15},{3,1}... | collective-permute-start | bytes 1671176 | tf_op jit(solution)/shard_map/ppermute | solution.py:385
  31.9 0.6 pad_add_fusion.at_ref
  32.5 4.0 %shard_map.87.begun_ref = bf16[4,13,32,1024]{3,2,1,0:T(8,128)(2,1)} custom-call(s32[4]{0:T(128)} %pad_add_fusion.at_ref, bf16[272,1024]{1,0:T(8,128)(2,1)} %shard_map.86.a_ref.i0, bf16[272,1024]{1,0:T(8,128)(2,1)} %copy-done.5), custom_call_target="tpu_custom_call" | custom-call | tf_op jit(solution)/shard_map/pallas_call | solution.py:359
  36.5 6.8 %collective-permute-done.2.a_ref.i0 = bf16[272,1024]{1,0:T(8,128)(2,1)S(1)} collective-permute-done((bf16[272,1024]{1,0:T(8,128)(2,1)S(1)}, bf16[272,1024]{1,0:T(8,128)(2,1)S(1)}, u32[]{:S(2)}, u32[]{:S(2)}) %collective-permute-start.2) | collective-permute-done | bytes 557088 | tf_op jit(solution)/shard_map/ppermute | solution.py:386
  43.3 0.8 copy-done.6
  44.2 4.0 %shard_map.88 = bf16[4,13,32,1024]{3,2,1,0:T(8,128)(2,1)} custom-call(s32[4]{0:T(128)} %pad_add_fusion.at_ref, bf16[272,1024]{1,0:T(8,128)(2,1)} %copy-done.4, bf16[272,1024]{1,0:T(8,128)(2,1)} %copy-done.6, bf16[4,13,32,1024]{3,2,1,0:T(8,128)(2,1)} %shard_map.87.begun_ref), custom_call_target="tpu_custom_call", output_to_operand_aliasing={{}: (3, {})} | custom-call | tf_op jit(solution)/shard_map/pallas_call | solution.py:359
  48.2 4.6 %shard_map.89 = f32[512,1024]{1,0:T(8,128)} custom-call(bf16[272,1024]{1,0:T(8,128)(2,1)} %shard_map.86.a_ref.i0, bf16[272,1024]{1,0:T(8,128)(2,1)} %copy-done.5, bf16[272,1024]{1,0:T(8,128)(2,1)} %copy-done.4, bf16[272,1024]{1,0:T(8,128)(2,1)} %copy-done.6, bf16[512,1024]{1,0:T(8,128)(2,1)} %all-gather.2.cloned.1.call-done.w_ref), custom_call_target="tpu_custom_call" | custom-call | tf_op jit(solution)/shard_map/pallas_call | solution.py:359
  52.9 0.0 reduce-scatter.6.cloned.1.call-update
  52.9 4.0 %all-to-all-start.1 = ((bf16[4,13,32,1024]{3,2,1,0:T(8,128)(2,1)}), bf16[4,13,32,1024]{3,2,1,0:T(8,128)(2,1)S(1)}, u32[]{:S(2)}, u32[]{:S(2)}) async-start(bf16[4,13,32,1024]{3,2,1,0:T(8,128)(2,1)} %shard_map.88), calls=%async_computation.1 | async-start | bytes 6815744 | tf_op jit(solution)/shard_map/all_to_all | solution.py:345
  56.9 2.5 %collective-permute-start = (bf16[8,1024,256]{2,1,0:T(8,128)(2,1)}, bf16[8,1024,256]{2,1,0:T(8,128)(2,1)}, u32[]{:S(2)}, u32[]{:S(2)}) collective-permute-start(bf16[8,1024,256]{2,1,0:T(8,128)(2,1)} %own_ref.3), channel_id=1, source_target_pairs={{0,1},{1,0},{2,3},{3,2},{4,5},{5,4},{6,7},{7,6},{8,9},{9,8},{10,11... | collective-permute-start | bytes 12582920 | tf_op jit(solution)/shard_map/ppermute | solution.py:387
  59.4 2.9 %collective-permute-start.7 = (bf16[272,1024]{1,0:T(8,128)(2,1)}, bf16[272,1024]{1,0:T(8,128)(2,1)S(1)}, u32[]{:S(2)}, u32[]{:S(2)}) collective-permute-start(bf16[272,1024]{1,0:T(8,128)(2,1)} %copy-done.6), channel_id=1, source_target_pairs={{0,14},{2,0},{4,2},{6,4},{8,6},{10,8},{12,10},{14,12},{1,15},{3,1}... | collective-permute-start | bytes 1671176 | tf_op jit(solution)/shard_map/ppermute | solution.py:385
  62.3 7.8 %collective-permute-done.3.a_ref.c_ref.i2 = bf16[272,1024]{1,0:T(8,128)(2,1)S(1)} collective-permute-done((bf16[272,1024]{1,0:T(8,128)(2,1)}, bf16[272,1024]{1,0:T(8,128)(2,1)S(1)}, u32[]{:S(2)}, u32[]{:S(2)}) %collective-permute-start.3) | collective-permute-done | bytes 557088 | tf_op jit(solution)/shard_map/ppermute | solution.py:386
  70.1 0.0 collective-permute-start.4
  70.1 4.6 %collective-permute-done.7.b_ref.i1 = bf16[272,1024]{1,0:T(8,128)(2,1)S(1)} collective-permute-done((bf16[272,1024]{1,0:T(8,128)(2,1)}, bf16[272,1024]{1,0:T(8,128)(2,1)S(1)}, u32[]{:S(2)}, u32[]{:S(2)}) %collective-permute-start.7) | collective-permute-done | bytes 557088 | tf_op jit(solution)/shard_map/ppermute | solution.py:385
  74.8 0.8 copy-done.8
  75.6 4.1 %shard_map.90.begun_ref = bf16[4,13,32,1024]{3,2,1,0:T(8,128)(2,1)} custom-call(s32[4]{0:T(128)} %pad_add_fusion.at_ref, bf16[272,1024]{1,0:T(8,128)(2,1)} %copy-done.3, bf16[272,1024]{1,0:T(8,128)(2,1)} %copy-done.8), custom_call_target="tpu_custom_call" | custom-call | tf_op jit(solution)/shard_map/pallas_call | solution.py:359
  79.7 2.7 %collective-permute-done.4.b_ref.d_ref.i3 = bf16[272,1024]{1,0:T(8,128)(2,1)S(1)} collective-permute-done((bf16[272,1024]{1,0:T(8,128)(2,1)S(1)}, bf16[272,1024]{1,0:T(8,128)(2,1)S(1)}, u32[]{:S(2)}, u32[]{:S(2)}) %collective-permute-start.4) | collective-permute-done | bytes 557088 | tf_op jit(solution)/shard_map/ppermute | solution.py:386
  82.3 0.8 copy-done.9
  83.1 4.0 %shard_map.91 = bf16[4,13,32,1024]{3,2,1,0:T(8,128)(2,1)} custom-call(s32[4]{0:T(128)} %pad_add_fusion.at_ref, bf16[272,1024]{1,0:T(8,128)(2,1)} %copy-done.7, bf16[272,1024]{1,0:T(8,128)(2,1)} %copy-done.9, bf16[4,13,32,1024]{3,2,1,0:T(8,128)(2,1)} %shard_map.90.begun_ref), custom_call_target="tpu_custom_call", output_to_operand_aliasing={{}: (3, {})} | custom-call | tf_op jit(solution)/shard_map/pallas_call | solution.py:359
  87.1 7.8 %all-to-all-done.1.r_ref.meta_ref = bf16[4,13,32,1024]{3,2,1,0:T(8,128)(2,1)S(1)} async-done(((bf16[4,13,32,1024]{3,2,1,0:T(8,128)(2,1)}), bf16[4,13,32,1024]{3,2,1,0:T(8,128)(2,1)S(1)}, u32[]{:S(2)}, u32[]{:S(2)}) %all-to-all-start.1) | async-done | bytes 3407904 | tf_op jit(solution)/shard_map/all_to_all | solution.py:345
  94.9 5.7 %shard_map.92 = f32[512,1024]{1,0:T(8,128)} custom-call(bf16[272,1024]{1,0:T(8,128)(2,1)} %copy-done.3, bf16[272,1024]{1,0:T(8,128)(2,1)} %copy-done.8, bf16[272,1024]{1,0:T(8,128)(2,1)} %copy-done.7, bf16[272,1024]{1,0:T(8,128)(2,1)} %copy-done.9, bf16[512,1024]{1,0:T(8,128)(2,1)} %all-gather.2.cloned.1.call-done.w_ref), custom_call_target="tpu_custom_call" | custom-call | tf_op jit(solution)/shard_map/pallas_call | solution.py:359
  100.6 0.0 reduce-scatter.4.cloned.1.call-update
  100.7 3.7 %all-to-all-start = ((bf16[4,13,32,1024]{3,2,1,0:T(8,128)(2,1)}), bf16[4,13,32,1024]{3,2,1,0:T(8,128)(2,1)S(1)}, u32[]{:S(2)}, u32[]{:S(2)}) async-start(bf16[4,13,32,1024]{3,2,1,0:T(8,128)(2,1)} %shard_map.91), calls=%async_computation | async-start | bytes 6815744 | tf_op jit(solution)/shard_map/all_to_all | solution.py:345
  104.4 0.0 reduce-scatter.8.cloned.1.call-start
  104.4 0.0 collective-permute-done.peer_ref
  104.5 10.1 %shard_map.93 = f32[4,2,6,32,256]{4,3,2,1,0:T(8,128)} custom-call(bf16[8,1024,256]{2,1,0:T(8,128)(2,1)} %own_ref.3, bf16[8,1024,256]{2,1,0:T(8,128)(2,1)} %collective-permute-done.peer_ref, bf16[4,13,32,1024]{3,2,1,0:T(8,128)(2,1)} %copy-done), custom_call_target="tpu_custom_call" | custom-call | flops 8000000000 | bytes 41943040 | tf_op jit(solution)/shard_map/pallas_call | solution.py:359
  114.6 0.0 reduce-scatter.8.cloned.1.call-update
  114.6 0.0 reduce-scatter.6.cloned.1.call-done.c_ref
  114.6 2.4 %shard_map.94.first_ref = f32[4,16,256]{2,1,0:T(8,128)} custom-call(s32[4]{0:T(128)} %pad_add_fusion.at_ref, f32[128,1024]{1,0:T(8,128)} %reduce-scatter.6.cloned.1.call-done.c_ref, bf16[272,1024]{1,0:T(8,128)(2,1)} %shard_map.86.a_ref.i0, bf16[272,1024]{1,0:T(8,128)(2,1)} %copy-done.5, bf16[272,1024]{1,0:T(8,128)(2,1)} %copy-done.4, bf16[272,1024]{1,0:T(8,128)(2,1)} %copy-done.6), custom_call_target="tpu_custom_call" | custom-call | tf_op jit(solution)/shard_map/pallas_call | solution.py:359
  117.0 16.3 %reduce-scatter.4.cloned.1.call-done.c_ref = f32[128,1024]{1,0:T(8,128)} async-done(((f32[512,1024]{1,0:T(8,128)}), f32[128,1024]{1,0:T(8,128)}) %reduce-scatter.4.cloned.1.call-update) | async-done | bytes 524304 | tf_op jit(solution)/shard_map/reduce_scatter | solution.py:437
  133.4 2.4 %shard_map.95 = (f32[16,256]{1,0:T(8,128)}, f32[16,256]{1,0:T(8,128)}, f32[16,256]{1,0:T(8,128)}, f32[16,256]{1,0:T(8,128)}, f32[16,256]{1,0:T(8,128)}, /*index=...) custom-call(s32[4]{0:T(128)} %pad_add_fusion.at_ref, f32[128,1024]{1,0:T(8,128)} %reduce-scatter.4.cloned.1.call-done.c_ref, ...), custom_call_target="tpu_custom_call" | custom-call | tf_op jit(solution)/shard_map/pallas_call | solution.py:359
  135.8 1.3 collective-permute-start.8
  137.1 1.8 collective-permute-start.9
  138.9 0.6 collective-permute-start.10
  139.5 1.9 all-to-all-done.r_ref.meta_ref
  141.4 0.0 collective-permute-done.8.refs_1_
  141.4 0.0 collective-permute-done.9.refs_2_
  141.4 2.7 %collective-permute-done.10.refs_3_ = f32[16,256]{1,0:T(8,128)S(1)} collective-permute-done((f32[16,256]{1,0:T(8,128)}, f32[16,256]{1,0:T(8,128)S(1)}, u32[]{:S(2)}, u32[]{:S(2)}) %collective-permute-start.10) | collective-permute-done | bytes 16416 | tf_op jit(solution)/shard_map/ppermute | solution.py:489
  144.2 10.5 %shard_map.96 = f32[4,2,6,32,256]{4,3,2,1,0:T(8,128)} custom-call(bf16[8,1024,256]{2,1,0:T(8,128)(2,1)} %own_ref.3, bf16[8,1024,256]{2,1,0:T(8,128)(2,1)} %collective-permute-done.peer_ref, bf16[4,13,32,1024]{3,2,1,0:T(8,128)(2,1)} %copy-done.1), custom_call_target="tpu_custom_call" | custom-call | flops 8000000000 | bytes 41943040 | tf_op jit(solution)/shard_map/pallas_call | solution.py:359
  154.7 3.6 %all-to-all-start.2 = ((f32[4,2,6,32,256]{4,3,2,1,0:T(8,128)}), f32[4,2,6,32,256]{4,3,2,1,0:T(8,128)S(1)}, u32[]{:S(2)}, u32[]{:S(2)}) async-start(f32[4,2,6,32,256]{4,3,2,1,0:T(8,128)} %shard_map.96), calls=%async_computation.4 | async-start | bytes 3145728 | tf_op jit(solution)/shard_map/all_to_all | solution.py:345
  158.3 1.2 collective-permute-start.11
  159.5 0.4 collective-permute-start.12
  159.9 4.1 %collective-permute-start.13 = (f32[16,256]{1,0:T(8,128)S(1)}, f32[16,256]{1,0:T(8,128)S(1)}, u32[]{:S(2)}, u32[]{:S(2)}) collective-permute-start(f32[16,256]{1,0:T(8,128)S(1)} %copy-done.21), channel_id=1, source_target_pairs={{0,10},{2,12},{4,14},{6,0},{8,2},{10,4},{12,6},{14,8},{1,11},{3,13... | collective-permute-start | bytes 49160 | tf_op jit(solution)/shard_map/ppermute | solution.py:489
  164.0 4.0 %collective-permute-start.14 = (f32[16,256]{1,0:T(8,128)S(1)}, f32[16,256]{1,0:T(8,128)S(1)}, u32[]{:S(2)}, u32[]{:S(2)}) collective-permute-start(f32[16,256]{1,0:T(8,128)S(1)} %copy-done.20), channel_id=1, source_target_pairs={{0,8},{2,10},{4,12},{6,14},{8,0},{10,2},{12,4},{14,6},{1,9},{3,11}... | collective-permute-start | bytes 49160 | tf_op jit(solution)/shard_map/ppermute | solution.py:489
  168.1 2.4 %collective-permute-done.14.refs_7_ = f32[16,256]{1,0:T(8,128)S(1)} collective-permute-done((f32[16,256]{1,0:T(8,128)S(1)}, f32[16,256]{1,0:T(8,128)S(1)}, u32[]{:S(2)}, u32[]{:S(2)}) %collective-permute-start.14) | collective-permute-done | bytes 16416 | tf_op jit(solution)/shard_map/ppermute | solution.py:489
  170.5 0.6 copy-done.16
  171.1 1.5 shard_map.97.refs_0_
  172.6 2.6 %collective-permute-start.17 = (f32[16,256]{1,0:T(8,128)}, f32[16,256]{1,0:T(8,128)S(1)}, u32[]{:S(2)}, u32[]{:S(2)}) collective-permute-start(f32[16,256]{1,0:T(8,128)} %shard_map.97.refs_0_), channel_id=1, source_target_pairs={{0,192},{64,0},{128,64},{192,128},{1,193},{65,1},{129,65},{193,129... | collective-permute-start | bytes 49160 | tf_op jit(solution)/shard_map/ppermute | solution.py:499
  175.2 1.8 collective-permute-start.15
  176.9 2.1 shard_map.98.first_ref
  179.1 1.1 collective-permute-done.16.refs_2_
  180.2 1.2 copy-done.2
  181.4 2.6 %shard_map.99 = f32[512,128]{1,0:T(8,128)} custom-call(s32[4]{0:T(128)} %pad_add_fusion.at_ref, f32[4,2,6,32,256]{4,3,2,1,0:T(8,128)} %copy-done.2, bf16[4,13,32,1024]{3,2,1,0:T(8,128)(2,1)} %copy-done.1, f32[8,256]{1,0:T(8,128)} %shard_map.98.first_ref), custom_call_target="tpu_custom_call" | custom-call | tf_op jit(solution)/shard_map/pallas_call | solution.py:359
  184.0 32.5 %all_to_all.26 = f32[256,2,128]{2,1,0:T(2,128)} all-to-all(f32[256,2,128]{2,1,0:T(2,128)} %bitcast.14), channel_id=1, replica_groups=mesh['hid'=4,'x'=4,'z'=8,'c'=2] {'hid','x','z','c'}, dimensions={0} | all-to-all | bytes 524288 | tf_op jit(solution)/shard_map/all_to_all | solution.py:345
  216.5 3.0 %shard_map.100 = (f32[1,256]{1,0:T(1,128)}, f32[8,256]{1,0:T(8,128)}) custom-call(s32[4]{0:T(128)} %pad_add_fusion.at_ref, f32[512,128]{1,0:T(8,128)} %bitcast.13, f32[16,256]{1,0:T(8,128)} %shard_map.97.refs_0_, f32[16,256]{1,0:T(8,128)} %copy-done.19, f32[16,256]{1,0:T(8,128)} %copy-done.18, f32[16,256]{1,0:T(8,128)} %copy-done.17, s32[8,256]{1,0:T(8,128)} %bitcast.17), custom_call_target="tpu_custom_call" | custom-call | tf_op jit(solution)/shard_map/pallas_call | solution.py:359
  (55 shorter events, 0.1 us)
Async XLA Ops:
  7.2 41.1 %all-gather.2.cloned.1.call-start = ((), (), s32[]{:S(2)}) async-start(), calls=%async_computation.7 | async-start | bytes 1179648 | tf_op jit(solution)/shard_map/all_gather | solution.py:388
  7.9 106.7 %reduce-scatter.6.cloned.1.call-start = ((), (), s32[]{:S(2)}) async-start(), calls=%async_computation.9 | async-start | bytes 2621440 | tf_op jit(solution)/shard_map/reduce_scatter | solution.py:437
  10.2 19.0 %collective-permute-start.1 = (bf16[272,1024]{1,0:T(8,128)(2,1)}, bf16[272,1024]{1,0:T(8,128)(2,1)S(1)}, u32[]{:S(2)}, u32[]{:S(2)}) collective-permute-start(bf16[272,1024]{1,0:T(8,128)(2,1)} %shard_map.86.a_ref.i0), channel_id=1, source_target_pairs={{0,2},{2,4},{4,6},{6,8},{8,10},{10,12},{12,14},{14,0},{1,3},{3,5},... | collective-permute-start | bytes 1671176 | tf_op jit(solution)/shard_map/ppermute | solution.py:386
  12.7 16.5 %collective-permute-start.5 = (bf16[272,1024]{1,0:T(8,128)(2,1)}, bf16[272,1024]{1,0:T(8,128)(2,1)S(1)}, u32[]{:S(2)}, u32[]{:S(2)}) collective-permute-start(bf16[272,1024]{1,0:T(8,128)(2,1)} %shard_map.86.a_ref.i0), channel_id=1, source_target_pairs={{0,14},{2,0},{4,2},{6,4},{8,6},{10,8},{12,10},{14,12},{1,15},{3,1}... | collective-permute-start | bytes 1671176 | tf_op jit(solution)/shard_map/ppermute | solution.py:385
  29.2 14.1 %copy-start.4 = (bf16[272,1024]{1,0:T(8,128)(2,1)}, bf16[272,1024]{1,0:T(8,128)(2,1)S(1)}, u32[]{:S(2)}) copy-start(bf16[272,1024]{1,0:T(8,128)(2,1)S(1)} %collective-permute-done.1.a_ref.c_ref.i2) | copy-start | bytes 1671172
  29.2 14.1 %collective-permute-start.2 = (bf16[272,1024]{1,0:T(8,128)(2,1)S(1)}, bf16[272,1024]{1,0:T(8,128)(2,1)S(1)}, u32[]{:S(2)}, u32[]{:S(2)}) collective-permute-start(bf16[272,1024]{1,0:T(8,128)(2,1)S(1)} %collective-permute-done.1.a_ref.c_ref.i2), channel_id=1, source_target_pairs={{0,2},{2,4},{4,6},{6,8},{8,10},{10,12},{12,14},{14,0},{1,3},{3,5},... | collective-permute-start | bytes 1671176 | tf_op jit(solution)/shard_map/ppermute | solution.py:386
  29.2 3.3 %copy-start.5 = (bf16[272,1024]{1,0:T(8,128)(2,1)}, bf16[272,1024]{1,0:T(8,128)(2,1)S(1)}, u32[]{:S(2)}) copy-start(bf16[272,1024]{1,0:T(8,128)(2,1)S(1)} %collective-permute-done.5.b_ref.i1) | copy-start | bytes 1671172
  29.2 14.1 %collective-permute-start.6 = (bf16[272,1024]{1,0:T(8,128)(2,1)S(1)}, bf16[272,1024]{1,0:T(8,128)(2,1)S(1)}, u32[]{:S(2)}, u32[]{:S(2)}) collective-permute-start(bf16[272,1024]{1,0:T(8,128)(2,1)S(1)} %collective-permute-done.5.b_ref.i1), channel_id=1, source_target_pairs={{0,14},{2,0},{4,2},{6,4},{8,6},{10,8},{12,10},{14,12},{1,15},{3,1}... | collective-permute-start | bytes 1671176 | tf_op jit(solution)/shard_map/ppermute | solution.py:385
  43.3 4.9 %copy-start.3 = (bf16[272,1024]{1,0:T(8,128)(2,1)}, bf16[272,1024]{1,0:T(8,128)(2,1)S(1)}, u32[]{:S(2)}) copy-start(bf16[272,1024]{1,0:T(8,128)(2,1)S(1)} %collective-permute-done.2.a_ref.i0) | copy-start | bytes 1671172
  43.3 0.8 copy-start.6
  52.9 42.0 %all-to-all-start.1 = ((bf16[4,13,32,1024]{3,2,1,0:T(8,128)(2,1)}), bf16[4,13,32,1024]{3,2,1,0:T(8,128)(2,1)S(1)}, u32[]{:S(2)}, u32[]{:S(2)}) async-start(bf16[4,13,32,1024]{3,2,1,0:T(8,128)(2,1)} %shard_map.88), calls=%async_computation.1 | async-start | bytes 6815744 | tf_op jit(solution)/shard_map/all_to_all | solution.py:345
  56.9 76.4 %reduce-scatter.4.cloned.1.call-start = ((), (), s32[]{:S(2)}) async-start(), calls=%async_computation.8 | async-start | bytes 2621440 | tf_op jit(solution)/shard_map/reduce_scatter | solution.py:437
  56.9 13.2 %collective-permute-start.3 = (bf16[272,1024]{1,0:T(8,128)(2,1)}, bf16[272,1024]{1,0:T(8,128)(2,1)S(1)}, u32[]{:S(2)}, u32[]{:S(2)}) collective-permute-start(bf16[272,1024]{1,0:T(8,128)(2,1)} %copy-done.3), channel_id=1, source_target_pairs={{0,2},{2,4},{4,6},{6,8},{8,10},{10,12},{12,14},{14,0},{1,3},{3,5},... | collective-permute-start | bytes 1671176 | tf_op jit(solution)/shard_map/ppermute | solution.py:386
  56.9 47.5 %collective-permute-start = (bf16[8,1024,256]{2,1,0:T(8,128)(2,1)}, bf16[8,1024,256]{2,1,0:T(8,128)(2,1)}, u32[]{:S(2)}, u32[]{:S(2)}) collective-permute-start(bf16[8,1024,256]{2,1,0:T(8,128)(2,1)} %own_ref.3), channel_id=1, source_target_pairs={{0,1},{1,0},{2,3},{3,2},{4,5},{5,4},{6,7},{7,6},{8,9},{9,8},{10,11... | collective-permute-start | bytes 12582920 | tf_op jit(solution)/shard_map/ppermute | solution.py:387
  59.4 15.3 %collective-permute-start.7 = (bf16[272,1024]{1,0:T(8,128)(2,1)}, bf16[272,1024]{1,0:T(8,128)(2,1)S(1)}, u32[]{:S(2)}, u32[]{:S(2)}) collective-permute-start(bf16[272,1024]{1,0:T(8,128)(2,1)} %copy-done.6), channel_id=1, source_target_pairs={{0,14},{2,0},{4,2},{6,4},{8,6},{10,8},{12,10},{14,12},{1,15},{3,1}... | collective-permute-start | bytes 1671176 | tf_op jit(solution)/shard_map/ppermute | solution.py:385
  70.1 12.2 %copy-start.7 = (bf16[272,1024]{1,0:T(8,128)(2,1)}, bf16[272,1024]{1,0:T(8,128)(2,1)S(1)}, u32[]{:S(2)}) copy-start(bf16[272,1024]{1,0:T(8,128)(2,1)S(1)} %collective-permute-done.3.a_ref.c_ref.i2) | copy-start | bytes 1671172
  70.1 12.2 %collective-permute-start.4 = (bf16[272,1024]{1,0:T(8,128)(2,1)S(1)}, bf16[272,1024]{1,0:T(8,128)(2,1)S(1)}, u32[]{:S(2)}, u32[]{:S(2)}) collective-permute-start(bf16[272,1024]{1,0:T(8,128)(2,1)S(1)} %collective-permute-done.3.a_ref.c_ref.i2), channel_id=1, source_target_pairs={{0,2},{2,4},{4,6},{6,8},{8,10},{10,12},{12,14},{14,0},{1,3},{3,5},... | collective-permute-start | bytes 1671176 | tf_op jit(solution)/shard_map/ppermute | solution.py:386
  74.8 0.8 copy-start.8
  82.3 0.8 copy-start.9
  94.9 5.8 %copy-start = (bf16[4,13,32,1024]{3,2,1,0:T(8,128)(2,1)}, bf16[4,13,32,1024]{3,2,1,0:T(8,128)(2,1)S(1)}, u32[]{:S(2)}) copy-start(bf16[4,13,32,1024]{3,2,1,0:T(8,128)(2,1)S(1)} %all-to-all-done.1.r_ref.meta_ref) | copy-start | bytes 10223620
  100.7 40.8 %all-to-all-start = ((bf16[4,13,32,1024]{3,2,1,0:T(8,128)(2,1)}), bf16[4,13,32,1024]{3,2,1,0:T(8,128)(2,1)S(1)}, u32[]{:S(2)}, u32[]{:S(2)}) async-start(bf16[4,13,32,1024]{3,2,1,0:T(8,128)(2,1)} %shard_map.91), calls=%async_computation | async-start | bytes 6815744 | tf_op jit(solution)/shard_map/all_to_all | solution.py:345
  104.4 72.5 %reduce-scatter.8.cloned.1.call-start = ((), (), s32[]{:S(2)}) async-start(), calls=%async_computation.10 | async-start | bytes 1966080 | tf_op jit(solution)/shard_map/reduce_scatter | solution.py:482
  135.8 5.6 %collective-permute-start.8 = (f32[16,256]{1,0:T(8,128)}, f32[16,256]{1,0:T(8,128)S(1)}, u32[]{:S(2)}, u32[]{:S(2)}) collective-permute-start(f32[16,256]{1,0:T(8,128)} %get-tuple-element.55), channel_id=1, source_target_pairs={{0,2},{2,4},{4,6},{6,8},{8,10},{10,12},{12,14},{14,0},{1,3},{3,5},... | collective-permute-start | bytes 49160 | tf_op jit(solution)/shard_map/ppermute | solution.py:489
  137.1 4.4 %collective-permute-start.9 = (f32[16,256]{1,0:T(8,128)}, f32[16,256]{1,0:T(8,128)S(1)}, u32[]{:S(2)}, u32[]{:S(2)}) collective-permute-start(f32[16,256]{1,0:T(8,128)} %get-tuple-element.56), channel_id=1, source_target_pairs={{0,14},{2,0},{4,2},{6,4},{8,6},{10,8},{12,10},{14,12},{1,15},{3,1}... | collective-permute-start | bytes 49160 | tf_op jit(solution)/shard_map/ppermute | solution.py:489
  138.9 5.3 %collective-permute-start.10 = (f32[16,256]{1,0:T(8,128)}, f32[16,256]{1,0:T(8,128)S(1)}, u32[]{:S(2)}, u32[]{:S(2)}) collective-permute-start(f32[16,256]{1,0:T(8,128)} %get-tuple-element.57), channel_id=1, source_target_pairs={{0,4},{2,6},{4,8},{6,10},{8,12},{10,14},{12,0},{14,2},{1,5},{3,7},... | collective-permute-start | bytes 49160 | tf_op jit(solution)/shard_map/ppermute | solution.py:489
  141.4 2.8 %copy-start.1 = (bf16[4,13,32,1024]{3,2,1,0:T(8,128)(2,1)}, bf16[4,13,32,1024]{3,2,1,0:T(8,128)(2,1)S(1)}, u32[]{:S(2)}) copy-start(bf16[4,13,32,1024]{3,2,1,0:T(8,128)(2,1)S(1)} %all-to-all-done.r_ref.meta_ref) | copy-start | bytes 10223620
  141.4 13.3 %copy-start.10 = (f32[16,256]{1,0:T(8,128)}, f32[16,256]{1,0:T(8,128)S(1)}, u32[]{:S(2)}) copy-start(f32[16,256]{1,0:T(8,128)S(1)} %collective-permute-done.8.refs_1_) | copy-start | bytes 49156
  141.4 13.3 %copy-start.11 = (f32[16,256]{1,0:T(8,128)}, f32[16,256]{1,0:T(8,128)S(1)}, u32[]{:S(2)}) copy-start(f32[16,256]{1,0:T(8,128)S(1)} %collective-permute-done.9.refs_2_) | copy-start | bytes 49156
  144.2 10.6 %copy-start.12 = (f32[16,256]{1,0:T(8,128)}, f32[16,256]{1,0:T(8,128)S(1)}, u32[]{:S(2)}) copy-start(f32[16,256]{1,0:T(8,128)S(1)} %collective-permute-done.10.refs_3_) | copy-start | bytes 49156
  144.2 14.1 %copy-start.23 = (f32[16,256]{1,0:T(8,128)S(1)}, f32[16,256]{1,0:T(8,128)}, u32[]{:S(2)}) copy-start(f32[16,256]{1,0:T(8,128)} %get-tuple-element.65) | copy-start | bytes 49156
  144.2 15.3 %copy-start.22 = (f32[16,256]{1,0:T(8,128)S(1)}, f32[16,256]{1,0:T(8,128)}, u32[]{:S(2)}) copy-start(f32[16,256]{1,0:T(8,128)} %get-tuple-element.66) | copy-start | bytes 49156
  144.2 15.7 %copy-start.21 = (f32[16,256]{1,0:T(8,128)S(1)}, f32[16,256]{1,0:T(8,128)}, u32[]{:S(2)}) copy-start(f32[16,256]{1,0:T(8,128)} %get-tuple-element.67) | copy-start | bytes 49156
  144.2 19.8 %copy-start.20 = (f32[16,256]{1,0:T(8,128)S(1)}, f32[16,256]{1,0:T(8,128)}, u32[]{:S(2)}) copy-start(f32[16,256]{1,0:T(8,128)} %get-tuple-element.68) | copy-start | bytes 49156
  154.7 25.4 %all-to-all-start.2 = ((f32[4,2,6,32,256]{4,3,2,1,0:T(8,128)}), f32[4,2,6,32,256]{4,3,2,1,0:T(8,128)S(1)}, u32[]{:S(2)}, u32[]{:S(2)}) async-start(f32[4,2,6,32,256]{4,3,2,1,0:T(8,128)} %shard_map.96), calls=%async_computation.4 | async-start | bytes 3145728 | tf_op jit(solution)/shard_map/all_to_all | solution.py:345
  158.3 9.7 %collective-permute-start.11 = (f32[16,256]{1,0:T(8,128)S(1)}, f32[16,256]{1,0:T(8,128)S(1)}, u32[]{:S(2)}, u32[]{:S(2)}) collective-permute-start(f32[16,256]{1,0:T(8,128)S(1)} %copy-done.23), channel_id=1, source_target_pairs={{0,12},{2,14},{4,0},{6,2},{8,4},{10,6},{12,8},{14,10},{1,13},{3,15... | collective-permute-start | bytes 49160 | tf_op jit(solution)/shard_map/ppermute | solution.py:489
  159.5 8.5 %collective-permute-start.12 = (f32[16,256]{1,0:T(8,128)S(1)}, f32[16,256]{1,0:T(8,128)S(1)}, u32[]{:S(2)}, u32[]{:S(2)}) collective-permute-start(f32[16,256]{1,0:T(8,128)S(1)} %copy-done.22), channel_id=1, source_target_pairs={{0,6},{2,8},{4,10},{6,12},{8,14},{10,0},{12,2},{14,4},{1,7},{3,9},... | collective-permute-start | bytes 49160 | tf_op jit(solution)/shard_map/ppermute | solution.py:489
  159.9 8.1 %collective-permute-start.13 = (f32[16,256]{1,0:T(8,128)S(1)}, f32[16,256]{1,0:T(8,128)S(1)}, u32[]{:S(2)}, u32[]{:S(2)}) collective-permute-start(f32[16,256]{1,0:T(8,128)S(1)} %copy-done.21), channel_id=1, source_target_pairs={{0,10},{2,12},{4,14},{6,0},{8,2},{10,4},{12,6},{14,8},{1,11},{3,13... | collective-permute-start | bytes 49160 | tf_op jit(solution)/shard_map/ppermute | solution.py:489
  164.0 6.5 %collective-permute-start.14 = (f32[16,256]{1,0:T(8,128)S(1)}, f32[16,256]{1,0:T(8,128)S(1)}, u32[]{:S(2)}, u32[]{:S(2)}) collective-permute-start(f32[16,256]{1,0:T(8,128)S(1)} %copy-done.20), channel_id=1, source_target_pairs={{0,8},{2,10},{4,12},{6,14},{8,0},{10,2},{12,4},{14,6},{1,9},{3,11}... | collective-permute-start | bytes 49160 | tf_op jit(solution)/shard_map/ppermute | solution.py:489
  168.0 2.5 %copy-start.13 = (f32[16,256]{1,0:T(8,128)}, f32[16,256]{1,0:T(8,128)S(1)}, u32[]{:S(2)}) copy-start(f32[16,256]{1,0:T(8,128)S(1)} %collective-permute-done.11.refs_4_) | copy-start | bytes 49156
  168.0 2.5 %copy-start.14 = (f32[16,256]{1,0:T(8,128)}, f32[16,256]{1,0:T(8,128)S(1)}, u32[]{:S(2)}) copy-start(f32[16,256]{1,0:T(8,128)S(1)} %collective-permute-done.12.refs_5_) | copy-start | bytes 49156
  168.1 2.5 %copy-start.15 = (f32[16,256]{1,0:T(8,128)}, f32[16,256]{1,0:T(8,128)S(1)}, u32[]{:S(2)}) copy-start(f32[16,256]{1,0:T(8,128)S(1)} %collective-permute-done.13.refs_6_) | copy-start | bytes 49156
  170.5 0.6 copy-start.16
  172.6 6.5 %collective-permute-start.17 = (f32[16,256]{1,0:T(8,128)}, f32[16,256]{1,0:T(8,128)S(1)}, u32[]{:S(2)}, u32[]{:S(2)}) collective-permute-start(f32[16,256]{1,0:T(8,128)} %shard_map.97.refs_0_), channel_id=1, source_target_pairs={{0,192},{64,0},{128,64},{192,128},{1,193},{65,1},{129,65},{193,129... | collective-permute-start | bytes 49160 | tf_op jit(solution)/shard_map/ppermute | solution.py:499
  175.2 5.0 %collective-permute-start.16 = (f32[16,256]{1,0:T(8,128)}, f32[16,256]{1,0:T(8,128)S(1)}, u32[]{:S(2)}, u32[]{:S(2)}) collective-permute-start(f32[16,256]{1,0:T(8,128)} %shard_map.97.refs_0_), channel_id=1, source_target_pairs={{0,64},{64,128},{128,192},{192,0},{1,65},{65,129},{129,193},{193,1... | collective-permute-start | bytes 49160 | tf_op jit(solution)/shard_map/ppermute | solution.py:499
  175.2 5.0 %collective-permute-start.15 = (f32[16,256]{1,0:T(8,128)}, f32[16,256]{1,0:T(8,128)S(1)}, u32[]{:S(2)}, u32[]{:S(2)}) collective-permute-start(f32[16,256]{1,0:T(8,128)} %shard_map.97.refs_0_), channel_id=1, source_target_pairs={{0,128},{64,192},{128,0},{192,64},{1,129},{65,193},{129,1},{193,65... | collective-permute-start | bytes 49160 | tf_op jit(solution)/shard_map/ppermute | solution.py:499
  179.1 37.4 %copy-start.17 = (f32[16,256]{1,0:T(8,128)}, f32[16,256]{1,0:T(8,128)S(1)}, u32[]{:S(2)}) copy-start(f32[16,256]{1,0:T(8,128)S(1)} %collective-permute-done.17.refs_3_) | copy-start | bytes 49156
  180.2 36.3 %copy-start.18 = (f32[16,256]{1,0:T(8,128)}, f32[16,256]{1,0:T(8,128)S(1)}, u32[]{:S(2)}) copy-start(f32[16,256]{1,0:T(8,128)S(1)} %collective-permute-done.16.refs_2_) | copy-start | bytes 49156
  180.2 36.3 %copy-start.19 = (f32[16,256]{1,0:T(8,128)}, f32[16,256]{1,0:T(8,128)S(1)}, u32[]{:S(2)}) copy-start(f32[16,256]{1,0:T(8,128)S(1)} %collective-permute-done.15.refs_1_) | copy-start | bytes 49156
  180.2 1.2 copy-start.2
Sparse Core Ops, SparseCore 0:
  9.9 30.0 all-gather.1
  53.0 33.7 reduce-scatter.5
  100.8 32.5 reduce-scatter.3
  135.8 26.9 reduce-scatter.7

commit v3 on v2

--- a/solution.py
+++ b/solution.py
@@ -489,7 +489,7 @@
         lax.ppermute(part, "z", [(i, (i + d) % NZ) for i in range(NZ)]) if d else part
         for part, d in zip(lines, away)
     ]
-    early = 4
+    early = NZ
     rows_far, *lines[:early] = lax.optimization_barrier((rows_far, *lines[:early]))
     fine_far = fine(rows_far)
     lines[0], _ = lax.optimization_barrier((lines[0], fine_far))

time: 227 us -> 230 us (1.013)
  waiting for transfers between devices: 67.5 us -> 71.3 us
  starting transfers between devices: 43.6 us -> 46.5 us
  blocking collectives: 32.5 us -> 30 us
    ppermute x3, waiting for transfers between devices: 1.12 us -> 10.4 us  [local(): lax.ppermute(own, 'hid', [(i, (i + d) % HID) for i in range(HID)])]
    ppermute x7, waiting for transfers between devices: 5.2 us -> 1.62 us  [local(): lax.ppermute(part, 'z', [(i, (i + d) % NZ) for i in range(NZ)])]
    ppermute x7, starting transfers between devices: 13.4 us -> 16.2 us  [local(): lax.ppermute(part, 'z', [(i, (i + d) % NZ) for i in range(NZ)])]
    all_to_all x1, blocking collectives: 32.5 us -> 30 us  [swap(): return lax.all_to_all(value, axes, split, split, tiled=True)]
  transfers between devices with their start and end apart: 25 -> 25, of which waited for: 11 -> 10; matrix products, arithmetic and copies ran while one was open for 0% -> 0% of each run, Pallas kernels for 24% -> 23%
where the time goes in v3:
time: 230 us; the launch traced here: 229 us
  waiting for transfers between devices  71.3 us (31%)
  Pallas kernels  63.2 us (27%)
  starting transfers between devices  46.5 us (20%)
  blocking collectives  30 us (13%)
  between operations  14 us (6%)
  local copies, waits for them, and re-layouts  3.83 us (2%)
    pallas_call x15, Pallas kernels, run(): pl.pallas_call(kernel, grid=(1,), in_specs=specs, out_specs=out_specs or...  63.2 us
    all_to_all x1, blocking collectives, swap(): return lax.all_to_all(value, axes, split, split, tiled=True)  30 us
    ppermute x4, waiting for transfers between devices, local(): from_down.append(lax.ppermute(from_down[-1], 'z', up))  29.8 us
    reduce_scatter x2, waiting for transfers between devices, partial(): return lax.psum_scatter(out, 'hid', scatter_dimension=0, tiled=True)  16.4 us
    ppermute x7, starting transfers between devices, local(): lax.ppermute(part, 'z', [(i, (i + d) % NZ) for i in range(NZ)])  16.2 us
    all_to_all x3, starting transfers between devices, swap(): return lax.all_to_all(value, axes, split, split, tiled=True)  11.3 us
    ppermute x3, waiting for transfers between devices, local(): lax.ppermute(own, 'hid', [(i, (i + d) % HID) for i in range(HID)])  10.4 us
    ppermute x3, starting transfers between devices, local(): from_up.append(lax.ppermute(from_up[-1], 'z', down))  9.47 us
  transfers between devices with their start and end apart: 25, of which 10 were waited for; matrix products, arithmetic and copies ran while one was open for 0% of the time, Pallas kernels for 23%

profile of v3, /device:TPU:1, one launch (start us, length us, event | category | flops | bytes accessed | tf_op | source)
XLA Modules:
  0.0 229.5 jit_solution(8090314638909058943)
XLA Ops:
  7.2 0.0 all-gather.2.cloned.1.call-start
  7.2 0.7 all-gather.2.cloned.1.call-update
  7.9 0.0 reduce-scatter.6.cloned.1.call-start
  7.9 2.3 shard_map.86.a_ref.i0
  10.2 2.5 %collective-permute-start.1 = (bf16[272,1024]{1,0:T(8,128)(2,1)}, bf16[272,1024]{1,0:T(8,128)(2,1)S(1)}, u32[]{:S(2)}, u32[]{:S(2)}) collective-permute-start(bf16[272,1024]{1,0:T(8,128)(2,1)} %shard_map.86.a_ref.i0), channel_id=1, source_target_pairs={{0,2},{2,4},{4,6},{6,8},{8,10},{10,12},{12,14},{14,0},{1,3},{3,5},... | collective-permute-start | bytes 1671176 | tf_op jit(solution)/shard_map/ppermute | solution.py:386
  12.7 3.9 %collective-permute-start.5 = (bf16[272,1024]{1,0:T(8,128)(2,1)}, bf16[272,1024]{1,0:T(8,128)(2,1)S(1)}, u32[]{:S(2)}, u32[]{:S(2)}) collective-permute-start(bf16[272,1024]{1,0:T(8,128)(2,1)} %shard_map.86.a_ref.i0), channel_id=1, source_target_pairs={{0,14},{2,0},{4,2},{6,4},{8,6},{10,8},{12,10},{14,12},{1,15},{3,1}... | collective-permute-start | bytes 1671176 | tf_op jit(solution)/shard_map/ppermute | solution.py:385
  16.6 12.6 %collective-permute-done.1.a_ref.c_ref.i2 = bf16[272,1024]{1,0:T(8,128)(2,1)S(1)} collective-permute-done((bf16[272,1024]{1,0:T(8,128)(2,1)}, bf16[272,1024]{1,0:T(8,128)(2,1)S(1)}, u32[]{:S(2)}, u32[]{:S(2)}) %collective-permute-start.1) | collective-permute-done | bytes 557088 | tf_op jit(solution)/shard_map/ppermute | solution.py:386
  29.2 0.0 collective-permute-start.2
  29.2 2.7 %collective-permute-start.6 = (bf16[272,1024]{1,0:T(8,128)(2,1)S(1)}, bf16[272,1024]{1,0:T(8,128)(2,1)S(1)}, u32[]{:S(2)}, u32[]{:S(2)}) collective-permute-start(bf16[272,1024]{1,0:T(8,128)(2,1)S(1)} %collective-permute-done.5.b_ref.i1), channel_id=1, source_target_pairs={{0,14},{2,0},{4,2},{6,4},{8,6},{10,8},{12,10},{14,12},{1,15},{3,1}... | collective-permute-start | bytes 1671176 | tf_op jit(solution)/shard_map/ppermute | solution.py:385
  31.9 0.7 pad_add_fusion.at_ref
  32.6 4.0 %shard_map.87.begun_ref = bf16[4,13,32,1024]{3,2,1,0:T(8,128)(2,1)} custom-call(s32[4]{0:T(128)} %pad_add_fusion.at_ref, bf16[272,1024]{1,0:T(8,128)(2,1)} %shard_map.86.a_ref.i0, bf16[272,1024]{1,0:T(8,128)(2,1)} %copy-done.5), custom_call_target="tpu_custom_call" | custom-call | tf_op jit(solution)/shard_map/pallas_call | solution.py:359
  36.6 6.7 %collective-permute-done.2.a_ref.i0 = bf16[272,1024]{1,0:T(8,128)(2,1)S(1)} collective-permute-done((bf16[272,1024]{1,0:T(8,128)(2,1)S(1)}, bf16[272,1024]{1,0:T(8,128)(2,1)S(1)}, u32[]{:S(2)}, u32[]{:S(2)}) %collective-permute-start.2) | collective-permute-done | bytes 557088 | tf_op jit(solution)/shard_map/ppermute | solution.py:386
  43.3 0.8 copy-done.6
  44.2 4.1 %shard_map.88 = bf16[4,13,32,1024]{3,2,1,0:T(8,128)(2,1)} custom-call(s32[4]{0:T(128)} %pad_add_fusion.at_ref, bf16[272,1024]{1,0:T(8,128)(2,1)} %copy-done.4, bf16[272,1024]{1,0:T(8,128)(2,1)} %copy-done.6, bf16[4,13,32,1024]{3,2,1,0:T(8,128)(2,1)} %shard_map.87.begun_ref), custom_call_target="tpu_custom_call", output_to_operand_aliasing={{}: (3, {})} | custom-call | tf_op jit(solution)/shard_map/pallas_call | solution.py:359
  48.2 4.6 %shard_map.89 = f32[512,1024]{1,0:T(8,128)} custom-call(bf16[272,1024]{1,0:T(8,128)(2,1)} %shard_map.86.a_ref.i0, bf16[272,1024]{1,0:T(8,128)(2,1)} %copy-done.5, bf16[272,1024]{1,0:T(8,128)(2,1)} %copy-done.4, bf16[272,1024]{1,0:T(8,128)(2,1)} %copy-done.6, bf16[512,1024]{1,0:T(8,128)(2,1)} %all-gather.2.cloned.1.call-done.w_ref), custom_call_target="tpu_custom_call" | custom-call | tf_op jit(solution)/shard_map/pallas_call | solution.py:359
  52.9 0.0 reduce-scatter.6.cloned.1.call-update
  52.9 4.0 %all-to-all-start.1 = ((bf16[4,13,32,1024]{3,2,1,0:T(8,128)(2,1)}), bf16[4,13,32,1024]{3,2,1,0:T(8,128)(2,1)S(1)}, u32[]{:S(2)}, u32[]{:S(2)}) async-start(bf16[4,13,32,1024]{3,2,1,0:T(8,128)(2,1)} %shard_map.88), calls=%async_computation.1 | async-start | bytes 6815744 | tf_op jit(solution)/shard_map/all_to_all | solution.py:345
  56.9 2.5 %collective-permute-start = (bf16[8,1024,256]{2,1,0:T(8,128)(2,1)}, bf16[8,1024,256]{2,1,0:T(8,128)(2,1)}, u32[]{:S(2)}, u32[]{:S(2)}) collective-permute-start(bf16[8,1024,256]{2,1,0:T(8,128)(2,1)} %own_ref.3), channel_id=1, source_target_pairs={{0,1},{1,0},{2,3},{3,2},{4,5},{5,4},{6,7},{7,6},{8,9},{9,8},{10,11... | collective-permute-start | bytes 12582920 | tf_op jit(solution)/shard_map/ppermute | solution.py:387
  59.4 2.9 %collective-permute-start.7 = (bf16[272,1024]{1,0:T(8,128)(2,1)}, bf16[272,1024]{1,0:T(8,128)(2,1)S(1)}, u32[]{:S(2)}, u32[]{:S(2)}) collective-permute-start(bf16[272,1024]{1,0:T(8,128)(2,1)} %copy-done.6), channel_id=1, source_target_pairs={{0,14},{2,0},{4,2},{6,4},{8,6},{10,8},{12,10},{14,12},{1,15},{3,1}... | collective-permute-start | bytes 1671176 | tf_op jit(solution)/shard_map/ppermute | solution.py:385
  62.3 7.8 %collective-permute-done.3.a_ref.c_ref.i2 = bf16[272,1024]{1,0:T(8,128)(2,1)S(1)} collective-permute-done((bf16[272,1024]{1,0:T(8,128)(2,1)}, bf16[272,1024]{1,0:T(8,128)(2,1)S(1)}, u32[]{:S(2)}, u32[]{:S(2)}) %collective-permute-start.3) | collective-permute-done | bytes 557088 | tf_op jit(solution)/shard_map/ppermute | solution.py:386
  70.1 0.0 collective-permute-start.4
  70.1 4.6 %collective-permute-done.7.b_ref.i1 = bf16[272,1024]{1,0:T(8,128)(2,1)S(1)} collective-permute-done((bf16[272,1024]{1,0:T(8,128)(2,1)}, bf16[272,1024]{1,0:T(8,128)(2,1)S(1)}, u32[]{:S(2)}, u32[]{:S(2)}) %collective-permute-start.7) | collective-permute-done | bytes 557088 | tf_op jit(solution)/shard_map/ppermute | solution.py:385
  74.8 0.8 copy-done.8
  75.6 4.1 %shard_map.90.begun_ref = bf16[4,13,32,1024]{3,2,1,0:T(8,128)(2,1)} custom-call(s32[4]{0:T(128)} %pad_add_fusion.at_ref, bf16[272,1024]{1,0:T(8,128)(2,1)} %copy-done.3, bf16[272,1024]{1,0:T(8,128)(2,1)} %copy-done.8), custom_call_target="tpu_custom_call" | custom-call | tf_op jit(solution)/shard_map/pallas_call | solution.py:359
  79.7 2.7 %collective-permute-done.4.b_ref.d_ref.i3 = bf16[272,1024]{1,0:T(8,128)(2,1)S(1)} collective-permute-done((bf16[272,1024]{1,0:T(8,128)(2,1)S(1)}, bf16[272,1024]{1,0:T(8,128)(2,1)S(1)}, u32[]{:S(2)}, u32[]{:S(2)}) %collective-permute-start.4) | collective-permute-done | bytes 557088 | tf_op jit(solution)/shard_map/ppermute | solution.py:386
  82.3 0.8 copy-done.9
  83.1 4.0 %shard_map.91 = bf16[4,13,32,1024]{3,2,1,0:T(8,128)(2,1)} custom-call(s32[4]{0:T(128)} %pad_add_fusion.at_ref, bf16[272,1024]{1,0:T(8,128)(2,1)} %copy-done.7, bf16[272,1024]{1,0:T(8,128)(2,1)} %copy-done.9, bf16[4,13,32,1024]{3,2,1,0:T(8,128)(2,1)} %shard_map.90.begun_ref), custom_call_target="tpu_custom_call", output_to_operand_aliasing={{}: (3, {})} | custom-call | tf_op jit(solution)/shard_map/pallas_call | solution.py:359
  87.1 7.8 %all-to-all-done.1.r_ref.meta_ref = bf16[4,13,32,1024]{3,2,1,0:T(8,128)(2,1)S(1)} async-done(((bf16[4,13,32,1024]{3,2,1,0:T(8,128)(2,1)}), bf16[4,13,32,1024]{3,2,1,0:T(8,128)(2,1)S(1)}, u32[]{:S(2)}, u32[]{:S(2)}) %all-to-all-start.1) | async-done | bytes 3407904 | tf_op jit(solution)/shard_map/all_to_all | solution.py:345
  94.9 5.7 %shard_map.92 = f32[512,1024]{1,0:T(8,128)} custom-call(bf16[272,1024]{1,0:T(8,128)(2,1)} %copy-done.3, bf16[272,1024]{1,0:T(8,128)(2,1)} %copy-done.8, bf16[272,1024]{1,0:T(8,128)(2,1)} %copy-done.7, bf16[272,1024]{1,0:T(8,128)(2,1)} %copy-done.9, bf16[512,1024]{1,0:T(8,128)(2,1)} %all-gather.2.cloned.1.call-done.w_ref), custom_call_target="tpu_custom_call" | custom-call | tf_op jit(solution)/shard_map/pallas_call | solution.py:359
  100.6 0.0 reduce-scatter.4.cloned.1.call-update
  100.6 3.7 %all-to-all-start = ((bf16[4,13,32,1024]{3,2,1,0:T(8,128)(2,1)}), bf16[4,13,32,1024]{3,2,1,0:T(8,128)(2,1)S(1)}, u32[]{:S(2)}, u32[]{:S(2)}) async-start(bf16[4,13,32,1024]{3,2,1,0:T(8,128)(2,1)} %shard_map.91), calls=%async_computation | async-start | bytes 6815744 | tf_op jit(solution)/shard_map/all_to_all | solution.py:345
  104.4 0.0 reduce-scatter.8.cloned.1.call-start
  104.4 0.0 collective-permute-done.peer_ref
  104.5 10.1 %shard_map.93 = f32[4,2,6,32,256]{4,3,2,1,0:T(8,128)} custom-call(bf16[8,1024,256]{2,1,0:T(8,128)(2,1)} %own_ref.3, bf16[8,1024,256]{2,1,0:T(8,128)(2,1)} %collective-permute-done.peer_ref, bf16[4,13,32,1024]{3,2,1,0:T(8,128)(2,1)} %copy-done), custom_call_target="tpu_custom_call" | custom-call | flops 8000000000 | bytes 41943040 | tf_op jit(solution)/shard_map/pallas_call | solution.py:359
  114.5 0.0 reduce-scatter.8.cloned.1.call-update
  114.6 0.0 reduce-scatter.6.cloned.1.call-done.c_ref
  114.6 2.4 %shard_map.94.first_ref = f32[4,16,256]{2,1,0:T(8,128)} custom-call(s32[4]{0:T(128)} %pad_add_fusion.at_ref, f32[128,1024]{1,0:T(8,128)} %reduce-scatter.6.cloned.1.call-done.c_ref, bf16[272,1024]{1,0:T(8,128)(2,1)} %shard_map.86.a_ref.i0, bf16[272,1024]{1,0:T(8,128)(2,1)} %copy-done.5, bf16[272,1024]{1,0:T(8,128)(2,1)} %copy-done.4, bf16[272,1024]{1,0:T(8,128)(2,1)} %copy-done.6), custom_call_target="tpu_custom_call" | custom-call | tf_op jit(solution)/shard_map/pallas_call | solution.py:359
  117.0 16.3 %reduce-scatter.4.cloned.1.call-done.c_ref = f32[128,1024]{1,0:T(8,128)} async-done(((f32[512,1024]{1,0:T(8,128)}), f32[128,1024]{1,0:T(8,128)}) %reduce-scatter.4.cloned.1.call-update) | async-done | bytes 524304 | tf_op jit(solution)/shard_map/reduce_scatter | solution.py:437
  133.4 2.4 %shard_map.95 = (f32[16,256]{1,0:T(8,128)}, f32[16,256]{1,0:T(8,128)}, f32[16,256]{1,0:T(8,128)}, f32[16,256]{1,0:T(8,128)}, f32[16,256]{1,0:T(8,128)}, /*index=...) custom-call(s32[4]{0:T(128)} %pad_add_fusion.at_ref, f32[128,1024]{1,0:T(8,128)} %reduce-scatter.4.cloned.1.call-done.c_ref, ...), custom_call_target="tpu_custom_call" | custom-call | tf_op jit(solution)/shard_map/pallas_call | solution.py:359
  135.8 1.3 collective-permute-start.8
  137.1 1.8 collective-permute-start.9
  138.9 0.6 collective-permute-start.10
  139.5 3.0 %collective-permute-start.11 = (f32[16,256]{1,0:T(8,128)}, f32[16,256]{1,0:T(8,128)S(1)}, u32[]{:S(2)}, u32[]{:S(2)}) collective-permute-start(f32[16,256]{1,0:T(8,128)} %get-tuple-element.62), channel_id=1, source_target_pairs={{0,12},{2,14},{4,0},{6,2},{8,4},{10,6},{12,8},{14,10},{1,13},{3,15... | collective-permute-start | bytes 49160 | tf_op jit(solution)/shard_map/ppermute | solution.py:489
  142.5 1.4 collective-permute-start.12
  143.9 3.1 %collective-permute-start.13 = (f32[16,256]{1,0:T(8,128)}, f32[16,256]{1,0:T(8,128)S(1)}, u32[]{:S(2)}, u32[]{:S(2)}) collective-permute-start(f32[16,256]{1,0:T(8,128)} %get-tuple-element.64), channel_id=1, source_target_pairs={{0,10},{2,12},{4,14},{6,0},{8,2},{10,4},{12,6},{14,8},{1,11},{3,13... | collective-permute-start | bytes 49160 | tf_op jit(solution)/shard_map/ppermute | solution.py:489
  147.0 5.0 %collective-permute-start.14 = (f32[16,256]{1,0:T(8,128)}, f32[16,256]{1,0:T(8,128)S(1)}, u32[]{:S(2)}, u32[]{:S(2)}) collective-permute-start(f32[16,256]{1,0:T(8,128)} %get-tuple-element.65), channel_id=1, source_target_pairs={{0,8},{2,10},{4,12},{6,14},{8,0},{10,2},{12,4},{14,6},{1,9},{3,11}... | collective-permute-start | bytes 49160 | tf_op jit(solution)/shard_map/ppermute | solution.py:489
  152.0 0.0 collective-permute-done.11.refs_4_
  152.1 1.6 collective-permute-done.14.refs_7_
  153.7 0.1 copy-done.1
  153.8 10.3 %shard_map.96 = f32[4,2,6,32,256]{4,3,2,1,0:T(8,128)} custom-call(bf16[8,1024,256]{2,1,0:T(8,128)(2,1)} %own_ref.3, bf16[8,1024,256]{2,1,0:T(8,128)(2,1)} %collective-permute-done.peer_ref, bf16[4,13,32,1024]{3,2,1,0:T(8,128)(2,1)} %copy-done.1), custom_call_target="tpu_custom_call" | custom-call | flops 8000000000 | bytes 41943040 | tf_op jit(solution)/shard_map/pallas_call | solution.py:359
  164.1 3.6 %all-to-all-start.2 = ((f32[4,2,6,32,256]{4,3,2,1,0:T(8,128)}), f32[4,2,6,32,256]{4,3,2,1,0:T(8,128)S(1)}, u32[]{:S(2)}, u32[]{:S(2)}) async-start(f32[4,2,6,32,256]{4,3,2,1,0:T(8,128)} %shard_map.96), calls=%async_computation.4 | async-start | bytes 3145728 | tf_op jit(solution)/shard_map/all_to_all | solution.py:345
  167.7 1.5 shard_map.97.refs_0_
  169.2 2.6 %collective-permute-start.17 = (f32[16,256]{1,0:T(8,128)}, f32[16,256]{1,0:T(8,128)S(1)}, u32[]{:S(2)}, u32[]{:S(2)}) collective-permute-start(f32[16,256]{1,0:T(8,128)} %shard_map.97.refs_0_), channel_id=1, source_target_pairs={{0,192},{64,0},{128,64},{192,128},{1,193},{65,1},{129,65},{193,129... | collective-permute-start | bytes 49160 | tf_op jit(solution)/shard_map/ppermute | solution.py:499
  171.8 0.0 collective-permute-start.16
  171.8 1.8 collective-permute-start.15
  173.6 2.1 shard_map.98.first_ref
  175.7 8.5 %collective-permute-done.17.refs_3_ = f32[16,256]{1,0:T(8,128)S(1)} collective-permute-done((f32[16,256]{1,0:T(8,128)}, f32[16,256]{1,0:T(8,128)S(1)}, u32[]{:S(2)}, u32[]{:S(2)}) %collective-permute-start.17) | collective-permute-done | bytes 16416 | tf_op jit(solution)/shard_map/ppermute | solution.py:499
  184.3 0.0 collective-permute-done.16.refs_2_
  184.3 1.9 collective-permute-done.15.refs_1_
  186.1 0.0 all-to-all-done.2.y_ref
  186.1 1.2 copy-done.2
  187.3 2.6 %shard_map.99 = f32[512,128]{1,0:T(8,128)} custom-call(s32[4]{0:T(128)} %pad_add_fusion.at_ref, f32[4,2,6,32,256]{4,3,2,1,0:T(8,128)} %copy-done.2, bf16[4,13,32,1024]{3,2,1,0:T(8,128)(2,1)} %copy-done.1, f32[8,256]{1,0:T(8,128)} %shard_map.98.first_ref), custom_call_target="tpu_custom_call" | custom-call | tf_op jit(solution)/shard_map/pallas_call | solution.py:359
  190.0 30.0 %all_to_all.26 = f32[256,2,128]{2,1,0:T(2,128)} all-to-all(f32[256,2,128]{2,1,0:T(2,128)} %bitcast.14), channel_id=1, replica_groups=mesh['hid'=4,'x'=4,'z'=8,'c'=2] {'hid','x','z','c'}, dimensions={0} | all-to-all | bytes 524288 | tf_op jit(solution)/shard_map/all_to_all | solution.py:345
  220.0 2.9 %shard_map.100 = (f32[1,256]{1,0:T(1,128)}, f32[8,256]{1,0:T(8,128)}) custom-call(s32[4]{0:T(128)} %pad_add_fusion.at_ref, f32[512,128]{1,0:T(8,128)} %bitcast.13, f32[16,256]{1,0:T(8,128)} %shard_map.97.refs_0_, f32[16,256]{1,0:T(8,128)} %copy-done.19, f32[16,256]{1,0:T(8,128)} %copy-done.18, f32[16,256]{1,0:T(8,128)} %copy-done.17, s32[8,256]{1,0:T(8,128)} %bitcast.17), custom_call_target="tpu_custom_call" | custom-call | tf_op jit(solution)/shard_map/pallas_call | solution.py:359
  (47 shorter events, 0.1 us)
Async XLA Ops:
  7.2 41.1 %all-gather.2.cloned.1.call-start = ((), (), s32[]{:S(2)}) async-start(), calls=%async_computation.7 | async-start | bytes 1179648 | tf_op jit(solution)/shard_map/all_gather | solution.py:388
  7.9 106.7 %reduce-scatter.6.cloned.1.call-start = ((), (), s32[]{:S(2)}) async-start(), calls=%async_computation.9 | async-start | bytes 2621440 | tf_op jit(solution)/shard_map/reduce_scatter | solution.py:437
  10.2 19.0 %collective-permute-start.1 = (bf16[272,1024]{1,0:T(8,128)(2,1)}, bf16[272,1024]{1,0:T(8,128)(2,1)S(1)}, u32[]{:S(2)}, u32[]{:S(2)}) collective-permute-start(bf16[272,1024]{1,0:T(8,128)(2,1)} %shard_map.86.a_ref.i0), channel_id=1, source_target_pairs={{0,2},{2,4},{4,6},{6,8},{8,10},{10,12},{12,14},{14,0},{1,3},{3,5},... | collective-permute-start | bytes 1671176 | tf_op jit(solution)/shard_map/ppermute | solution.py:386
  12.7 16.5 %collective-permute-start.5 = (bf16[272,1024]{1,0:T(8,128)(2,1)}, bf16[272,1024]{1,0:T(8,128)(2,1)S(1)}, u32[]{:S(2)}, u32[]{:S(2)}) collective-permute-start(bf16[272,1024]{1,0:T(8,128)(2,1)} %shard_map.86.a_ref.i0), channel_id=1, source_target_pairs={{0,14},{2,0},{4,2},{6,4},{8,6},{10,8},{12,10},{14,12},{1,15},{3,1}... | collective-permute-start | bytes 1671176 | tf_op jit(solution)/shard_map/ppermute | solution.py:385
  29.2 14.1 %copy-start.4 = (bf16[272,1024]{1,0:T(8,128)(2,1)}, bf16[272,1024]{1,0:T(8,128)(2,1)S(1)}, u32[]{:S(2)}) copy-start(bf16[272,1024]{1,0:T(8,128)(2,1)S(1)} %collective-permute-done.1.a_ref.c_ref.i2) | copy-start | bytes 1671172
  29.2 14.1 %collective-permute-start.2 = (bf16[272,1024]{1,0:T(8,128)(2,1)S(1)}, bf16[272,1024]{1,0:T(8,128)(2,1)S(1)}, u32[]{:S(2)}, u32[]{:S(2)}) collective-permute-start(bf16[272,1024]{1,0:T(8,128)(2,1)S(1)} %collective-permute-done.1.a_ref.c_ref.i2), channel_id=1, source_target_pairs={{0,2},{2,4},{4,6},{6,8},{8,10},{10,12},{12,14},{14,0},{1,3},{3,5},... | collective-permute-start | bytes 1671176 | tf_op jit(solution)/shard_map/ppermute | solution.py:386
  29.2 3.3 %copy-start.5 = (bf16[272,1024]{1,0:T(8,128)(2,1)}, bf16[272,1024]{1,0:T(8,128)(2,1)S(1)}, u32[]{:S(2)}) copy-start(bf16[272,1024]{1,0:T(8,128)(2,1)S(1)} %collective-permute-done.5.b_ref.i1) | copy-start | bytes 1671172
  29.2 14.1 %collective-permute-start.6 = (bf16[272,1024]{1,0:T(8,128)(2,1)S(1)}, bf16[272,1024]{1,0:T(8,128)(2,1)S(1)}, u32[]{:S(2)}, u32[]{:S(2)}) collective-permute-start(bf16[272,1024]{1,0:T(8,128)(2,1)S(1)} %collective-permute-done.5.b_ref.i1), channel_id=1, source_target_pairs={{0,14},{2,0},{4,2},{6,4},{8,6},{10,8},{12,10},{14,12},{1,15},{3,1}... | collective-permute-start | bytes 1671176 | tf_op jit(solution)/shard_map/ppermute | solution.py:385
  43.3 4.9 %copy-start.3 = (bf16[272,1024]{1,0:T(8,128)(2,1)}, bf16[272,1024]{1,0:T(8,128)(2,1)S(1)}, u32[]{:S(2)}) copy-start(bf16[272,1024]{1,0:T(8,128)(2,1)S(1)} %collective-permute-done.2.a_ref.i0) | copy-start | bytes 1671172
  43.3 0.8 copy-start.6
  52.9 42.0 %all-to-all-start.1 = ((bf16[4,13,32,1024]{3,2,1,0:T(8,128)(2,1)}), bf16[4,13,32,1024]{3,2,1,0:T(8,128)(2,1)S(1)}, u32[]{:S(2)}, u32[]{:S(2)}) async-start(bf16[4,13,32,1024]{3,2,1,0:T(8,128)(2,1)} %shard_map.88), calls=%async_computation.1 | async-start | bytes 6815744 | tf_op jit(solution)/shard_map/all_to_all | solution.py:345
  56.9 76.4 %reduce-scatter.4.cloned.1.call-start = ((), (), s32[]{:S(2)}) async-start(), calls=%async_computation.8 | async-start | bytes 2621440 | tf_op jit(solution)/shard_map/reduce_scatter | solution.py:437
  56.9 13.2 %collective-permute-start.3 = (bf16[272,1024]{1,0:T(8,128)(2,1)}, bf16[272,1024]{1,0:T(8,128)(2,1)S(1)}, u32[]{:S(2)}, u32[]{:S(2)}) collective-permute-start(bf16[272,1024]{1,0:T(8,128)(2,1)} %copy-done.3), channel_id=1, source_target_pairs={{0,2},{2,4},{4,6},{6,8},{8,10},{10,12},{12,14},{14,0},{1,3},{3,5},... | collective-permute-start | bytes 1671176 | tf_op jit(solution)/shard_map/ppermute | solution.py:386
  56.9 47.5 %collective-permute-start = (bf16[8,1024,256]{2,1,0:T(8,128)(2,1)}, bf16[8,1024,256]{2,1,0:T(8,128)(2,1)}, u32[]{:S(2)}, u32[]{:S(2)}) collective-permute-start(bf16[8,1024,256]{2,1,0:T(8,128)(2,1)} %own_ref.3), channel_id=1, source_target_pairs={{0,1},{1,0},{2,3},{3,2},{4,5},{5,4},{6,7},{7,6},{8,9},{9,8},{10,11... | collective-permute-start | bytes 12582920 | tf_op jit(solution)/shard_map/ppermute | solution.py:387
  59.4 15.3 %collective-permute-start.7 = (bf16[272,1024]{1,0:T(8,128)(2,1)}, bf16[272,1024]{1,0:T(8,128)(2,1)S(1)}, u32[]{:S(2)}, u32[]{:S(2)}) collective-permute-start(bf16[272,1024]{1,0:T(8,128)(2,1)} %copy-done.6), channel_id=1, source_target_pairs={{0,14},{2,0},{4,2},{6,4},{8,6},{10,8},{12,10},{14,12},{1,15},{3,1}... | collective-permute-start | bytes 1671176 | tf_op jit(solution)/shard_map/ppermute | solution.py:385
  70.1 12.2 %copy-start.7 = (bf16[272,1024]{1,0:T(8,128)(2,1)}, bf16[272,1024]{1,0:T(8,128)(2,1)S(1)}, u32[]{:S(2)}) copy-start(bf16[272,1024]{1,0:T(8,128)(2,1)S(1)} %collective-permute-done.3.a_ref.c_ref.i2) | copy-start | bytes 1671172
  70.1 12.2 %collective-permute-start.4 = (bf16[272,1024]{1,0:T(8,128)(2,1)S(1)}, bf16[272,1024]{1,0:T(8,128)(2,1)S(1)}, u32[]{:S(2)}, u32[]{:S(2)}) collective-permute-start(bf16[272,1024]{1,0:T(8,128)(2,1)S(1)} %collective-permute-done.3.a_ref.c_ref.i2), channel_id=1, source_target_pairs={{0,2},{2,4},{4,6},{6,8},{8,10},{10,12},{12,14},{14,0},{1,3},{3,5},... | collective-permute-start | bytes 1671176 | tf_op jit(solution)/shard_map/ppermute | solution.py:386
  74.8 0.8 copy-start.8
  82.3 0.8 copy-start.9
  94.9 5.8 %copy-start = (bf16[4,13,32,1024]{3,2,1,0:T(8,128)(2,1)}, bf16[4,13,32,1024]{3,2,1,0:T(8,128)(2,1)S(1)}, u32[]{:S(2)}) copy-start(bf16[4,13,32,1024]{3,2,1,0:T(8,128)(2,1)S(1)} %all-to-all-done.1.r_ref.meta_ref) | copy-start | bytes 10223620
  100.6 51.3 %all-to-all-start = ((bf16[4,13,32,1024]{3,2,1,0:T(8,128)(2,1)}), bf16[4,13,32,1024]{3,2,1,0:T(8,128)(2,1)S(1)}, u32[]{:S(2)}, u32[]{:S(2)}) async-start(bf16[4,13,32,1024]{3,2,1,0:T(8,128)(2,1)} %shard_map.91), calls=%async_computation | async-start | bytes 6815744 | tf_op jit(solution)/shard_map/all_to_all | solution.py:345
  104.4 69.2 %reduce-scatter.8.cloned.1.call-start = ((), (), s32[]{:S(2)}) async-start(), calls=%async_computation.10 | async-start | bytes 1966080 | tf_op jit(solution)/shard_map/reduce_scatter | solution.py:482
  135.8 8.1 %collective-permute-start.8 = (f32[16,256]{1,0:T(8,128)}, f32[16,256]{1,0:T(8,128)S(1)}, u32[]{:S(2)}, u32[]{:S(2)}) collective-permute-start(f32[16,256]{1,0:T(8,128)} %get-tuple-element.59), channel_id=1, source_target_pairs={{0,2},{2,4},{4,6},{6,8},{8,10},{10,12},{12,14},{14,0},{1,3},{3,5},... | collective-permute-start | bytes 49160 | tf_op jit(solution)/shard_map/ppermute | solution.py:489
  137.1 9.9 %collective-permute-start.9 = (f32[16,256]{1,0:T(8,128)}, f32[16,256]{1,0:T(8,128)S(1)}, u32[]{:S(2)}, u32[]{:S(2)}) collective-permute-start(f32[16,256]{1,0:T(8,128)} %get-tuple-element.60), channel_id=1, source_target_pairs={{0,14},{2,0},{4,2},{6,4},{8,6},{10,8},{12,10},{14,12},{1,15},{3,1}... | collective-permute-start | bytes 49160 | tf_op jit(solution)/shard_map/ppermute | solution.py:489
  138.9 13.1 %collective-permute-start.10 = (f32[16,256]{1,0:T(8,128)}, f32[16,256]{1,0:T(8,128)S(1)}, u32[]{:S(2)}, u32[]{:S(2)}) collective-permute-start(f32[16,256]{1,0:T(8,128)} %get-tuple-element.61), channel_id=1, source_target_pairs={{0,4},{2,6},{4,8},{6,10},{8,12},{10,14},{12,0},{14,2},{1,5},{3,7},... | collective-permute-start | bytes 49160 | tf_op jit(solution)/shard_map/ppermute | solution.py:489
  139.5 12.5 %collective-permute-start.11 = (f32[16,256]{1,0:T(8,128)}, f32[16,256]{1,0:T(8,128)S(1)}, u32[]{:S(2)}, u32[]{:S(2)}) collective-permute-start(f32[16,256]{1,0:T(8,128)} %get-tuple-element.62), channel_id=1, source_target_pairs={{0,12},{2,14},{4,0},{6,2},{8,4},{10,6},{12,8},{14,10},{1,13},{3,15... | collective-permute-start | bytes 49160 | tf_op jit(solution)/shard_map/ppermute | solution.py:489
  142.5 9.5 %collective-permute-start.12 = (f32[16,256]{1,0:T(8,128)}, f32[16,256]{1,0:T(8,128)S(1)}, u32[]{:S(2)}, u32[]{:S(2)}) collective-permute-start(f32[16,256]{1,0:T(8,128)} %get-tuple-element.63), channel_id=1, source_target_pairs={{0,6},{2,8},{4,10},{6,12},{8,14},{10,0},{12,2},{14,4},{1,7},{3,9},... | collective-permute-start | bytes 49160 | tf_op jit(solution)/shard_map/ppermute | solution.py:489
  143.9 20.2 %copy-start.10 = (f32[16,256]{1,0:T(8,128)}, f32[16,256]{1,0:T(8,128)S(1)}, u32[]{:S(2)}) copy-start(f32[16,256]{1,0:T(8,128)S(1)} %collective-permute-done.8.refs_1_) | copy-start | bytes 49156
  143.9 8.1 %collective-permute-start.13 = (f32[16,256]{1,0:T(8,128)}, f32[16,256]{1,0:T(8,128)S(1)}, u32[]{:S(2)}, u32[]{:S(2)}) collective-permute-start(f32[16,256]{1,0:T(8,128)} %get-tuple-element.64), channel_id=1, source_target_pairs={{0,10},{2,12},{4,14},{6,0},{8,2},{10,4},{12,6},{14,8},{1,11},{3,13... | collective-permute-start | bytes 49160 | tf_op jit(solution)/shard_map/ppermute | solution.py:489
  147.0 17.1 %copy-start.11 = (f32[16,256]{1,0:T(8,128)}, f32[16,256]{1,0:T(8,128)S(1)}, u32[]{:S(2)}) copy-start(f32[16,256]{1,0:T(8,128)S(1)} %collective-permute-done.9.refs_2_) | copy-start | bytes 49156
  147.0 6.7 %collective-permute-start.14 = (f32[16,256]{1,0:T(8,128)}, f32[16,256]{1,0:T(8,128)S(1)}, u32[]{:S(2)}, u32[]{:S(2)}) collective-permute-start(f32[16,256]{1,0:T(8,128)} %get-tuple-element.65), channel_id=1, source_target_pairs={{0,8},{2,10},{4,12},{6,14},{8,0},{10,2},{12,4},{14,6},{1,9},{3,11}... | collective-permute-start | bytes 49160 | tf_op jit(solution)/shard_map/ppermute | solution.py:489
  152.0 1.8 copy-start.1
  152.0 12.1 %copy-start.12 = (f32[16,256]{1,0:T(8,128)}, f32[16,256]{1,0:T(8,128)S(1)}, u32[]{:S(2)}) copy-start(f32[16,256]{1,0:T(8,128)S(1)} %collective-permute-done.10.refs_3_) | copy-start | bytes 49156
  152.0 12.1 %copy-start.13 = (f32[16,256]{1,0:T(8,128)}, f32[16,256]{1,0:T(8,128)S(1)}, u32[]{:S(2)}) copy-start(f32[16,256]{1,0:T(8,128)S(1)} %collective-permute-done.11.refs_4_) | copy-start | bytes 49156
  152.0 12.1 %copy-start.14 = (f32[16,256]{1,0:T(8,128)}, f32[16,256]{1,0:T(8,128)S(1)}, u32[]{:S(2)}) copy-start(f32[16,256]{1,0:T(8,128)S(1)} %collective-permute-done.12.refs_5_) | copy-start | bytes 49156
  152.0 12.1 %copy-start.15 = (f32[16,256]{1,0:T(8,128)}, f32[16,256]{1,0:T(8,128)S(1)}, u32[]{:S(2)}) copy-start(f32[16,256]{1,0:T(8,128)S(1)} %collective-permute-done.13.refs_6_) | copy-start | bytes 49156
  153.7 10.5 %copy-start.16 = (f32[16,256]{1,0:T(8,128)}, f32[16,256]{1,0:T(8,128)S(1)}, u32[]{:S(2)}) copy-start(f32[16,256]{1,0:T(8,128)S(1)} %collective-permute-done.14.refs_7_) | copy-start | bytes 49156
  164.1 22.0 %all-to-all-start.2 = ((f32[4,2,6,32,256]{4,3,2,1,0:T(8,128)}), f32[4,2,6,32,256]{4,3,2,1,0:T(8,128)S(1)}, u32[]{:S(2)}, u32[]{:S(2)}) async-start(f32[4,2,6,32,256]{4,3,2,1,0:T(8,128)} %shard_map.96), calls=%async_computation.4 | async-start | bytes 3145728 | tf_op jit(solution)/shard_map/all_to_all | solution.py:345
  169.2 15.1 %collective-permute-start.17 = (f32[16,256]{1,0:T(8,128)}, f32[16,256]{1,0:T(8,128)S(1)}, u32[]{:S(2)}, u32[]{:S(2)}) collective-permute-start(f32[16,256]{1,0:T(8,128)} %shard_map.97.refs_0_), channel_id=1, source_target_pairs={{0,192},{64,0},{128,64},{192,128},{1,193},{65,1},{129,65},{193,129... | collective-permute-start | bytes 49160 | tf_op jit(solution)/shard_map/ppermute | solution.py:499
  171.8 12.4 %collective-permute-start.16 = (f32[16,256]{1,0:T(8,128)}, f32[16,256]{1,0:T(8,128)S(1)}, u32[]{:S(2)}, u32[]{:S(2)}) collective-permute-start(f32[16,256]{1,0:T(8,128)} %shard_map.97.refs_0_), channel_id=1, source_target_pairs={{0,64},{64,128},{128,192},{192,0},{1,65},{65,129},{129,193},{193,1... | collective-permute-start | bytes 49160 | tf_op jit(solution)/shard_map/ppermute | solution.py:499
  171.8 14.3 %collective-permute-start.15 = (f32[16,256]{1,0:T(8,128)}, f32[16,256]{1,0:T(8,128)S(1)}, u32[]{:S(2)}, u32[]{:S(2)}) collective-permute-start(f32[16,256]{1,0:T(8,128)} %shard_map.97.refs_0_), channel_id=1, source_target_pairs={{0,128},{64,192},{128,0},{192,64},{1,129},{65,193},{129,1},{193,65... | collective-permute-start | bytes 49160 | tf_op jit(solution)/shard_map/ppermute | solution.py:499
  184.3 35.7 %copy-start.17 = (f32[16,256]{1,0:T(8,128)}, f32[16,256]{1,0:T(8,128)S(1)}, u32[]{:S(2)}) copy-start(f32[16,256]{1,0:T(8,128)S(1)} %collective-permute-done.17.refs_3_) | copy-start | bytes 49156
  184.3 35.7 %copy-start.18 = (f32[16,256]{1,0:T(8,128)}, f32[16,256]{1,0:T(8,128)S(1)}, u32[]{:S(2)}) copy-start(f32[16,256]{1,0:T(8,128)S(1)} %collective-permute-done.16.refs_2_) | copy-start | bytes 49156
  186.1 33.8 %copy-start.19 = (f32[16,256]{1,0:T(8,128)}, f32[16,256]{1,0:T(8,128)S(1)}, u32[]{:S(2)}) copy-start(f32[16,256]{1,0:T(8,128)S(1)} %collective-permute-done.15.refs_1_) | copy-start | bytes 49156
  186.1 1.2 copy-start.2
Sparse Core Ops, SparseCore 0:
  9.9 30.0 all-gather.1
  53.0 33.7 reduce-scatter.5
  100.8 32.5 reduce-scatter.3
  135.8 27.0 reduce-scatter.7
